TPU v7x, 256 devices: a whole 4x4x8 slice. The times are simulated.
256 devices in a mesh: seq: 128 (over z, y, x), ch: 2 (over core).
Axes of the slice: x: 4, y: 4, z: 8, core: 2. Of those that a mesh axis runs over, the one named last changes fastest.
Arguments:
- conv_in: bfloat16 [32768, 4096], P('seq', 'ch'), may hold values from -6 to 6
- norm_gain: float32 [4096], P('ch'), may hold values from 0.25 to 1.75
- filters: bfloat16 [256, 128], P('ch'), may hold values from -0.5 to 0.5
- gate: bfloat16 [32768, 4096], P('seq', 'ch'), may hold values from -6 to 6
- queries: bfloat16 [32768, 4096], P('seq', 'ch'), may hold values from -90 to 90
- keys: bfloat16 [32768, 4096], P('seq', 'ch'), may hold values from -6 to 6
- doc_lengths: int32 [48], replicated, may hold values from 1 to 768, 32768 in all
Outputs:
- mixed: bfloat16 [32768, 4096], P('seq', 'ch')
- attended: bfloat16 [32768, 4096], P('seq', 'ch')
Inputs may be any that keep to these rules, and one draw needn't show every extreme that they name: `doc_lengths`: no document is longer than 768 tokens, and one has exactly that many; the lengths sum to 32768.
All inputs are finite; a program needn't handle non-finite values.
Results may differ from a plain program's by a relative error of at most 0.0065.
Values may be sent and summed in bfloat16 or wider, within the bound.
No kernel may reach another device: no remote copies, remote signals or barrier semaphores. Data moves between devices by JAX's collectives and lax.ppermute only.
A program may use at most 128 MiB of HBM per device.

v0:
```python
import jax
import jax.numpy as jnp
from jax import lax
from jax.sharding import PartitionSpec as P

HEAD_DIM = 128
SPAN = 4
CONV_CH = 4096


def from_behind(value, axis, steps):
    count = lax.axis_size(axis)
    initial, last = (max(0, -steps), min(count, count - steps))
    return lax.ppermute(value, axis, [(source, source + steps) for source in range(initial, last)])


def begin_of(doc_lengths, positions):
    ends = jnp.cumsum(doc_lengths)
    starts = ends - doc_lengths
    inside = starts[None, :] <= positions[:, None]
    return jnp.max(jnp.where(inside, starts[None, :], 0), axis=1)


def band_taps(filters):
    taps_count = filters.shape[1]
    out_idx = jnp.arange(taps_count, dtype=jnp.int32)
    src_idx = jnp.arange(2 * taps_count, dtype=jnp.int32)
    lag = out_idx[:, None] - src_idx[None, :] + taps_count
    onehot = (lag[:, :, None] == out_idx[None, None, :]).astype(jnp.bfloat16)
    taps = jnp.einsum("nml,gl->gnm", onehot, filters, preferred_element_type=jnp.float32)
    return taps.astype(jnp.bfloat16)


def shards(conv_in, norm_gain, filters, gate, queries, keys, doc_lengths):
    rows, width = conv_in.shape
    taps_count = filters.shape[1]
    groups_dev = filters.shape[0]
    heads_dev = width // HEAD_DIM
    base = lax.axis_index("seq") * rows
    positions = base + jnp.arange(rows, dtype=jnp.int32)
    begin = begin_of(doc_lengths, positions)
    wide = conv_in.astype(jnp.float32)
    energy = lax.psum(jnp.sum(wide * wide, axis=1), "ch")
    normed = (wide * lax.rsqrt(energy / CONV_CH + 1e-06)[:, None] * norm_gain[None, :]).astype(
        jnp.bfloat16
    )
    tail = from_behind(normed[rows - taps_count :], "seq", 1)
    source = jnp.concatenate([tail, normed], axis=0)
    banded = band_taps(filters)
    pieces = []
    for block in range(rows // taps_count):
        low = block * taps_count
        src_rows = source[low : low + 2 * taps_count]
        src_pos = base - taps_count + low + jnp.arange(2 * taps_count, dtype=jnp.int32)
        inside = src_pos[None, :] >= begin[low : low + taps_count][:, None]
        matrix = jnp.where(inside[None], banded, jnp.zeros_like(banded))
        filt = jnp.einsum(
            "gnm,mgc->ngc",
            matrix,
            src_rows.reshape(2 * taps_count, groups_dev, -1),
            preferred_element_type=jnp.float32,
        )
        gated = gate[low : low + taps_count].astype(jnp.float32)
        pieces.append((gated * filt.reshape(taps_count, width)).astype(jnp.bfloat16))
    mixed = jnp.concatenate(pieces, axis=0)
    query = queries.reshape(rows, heads_dev, HEAD_DIM)
    scale = HEAD_DIM ** (-0.5)

    def accumulate(carry, pair, back):
        top, total, acc = carry
        key_blk = pair[0].reshape(rows, heads_dev, HEAD_DIM)
        val_blk = pair[1].reshape(rows, heads_dev, HEAD_DIM)
        kpos = base - back * rows + jnp.arange(rows, dtype=jnp.int32)
        valid = (kpos[None, :] <= positions[:, None]) & (kpos[None, :] >= begin[:, None])
        score = (
            jnp.einsum("rhd,khd->hrk", query, key_blk, preferred_element_type=jnp.float32) * scale
        )
        score = jnp.where(valid[None], score, -1e30)
        new_top = jnp.maximum(top, jnp.max(score, axis=2))
        weight = jnp.where(valid[None], jnp.exp(score - new_top[:, :, None]), 0.0)
        factor = jnp.exp(top - new_top)
        total = total * factor + jnp.sum(weight, axis=2)
        update = jnp.einsum(
            "hrk,khd->hrd", weight.astype(jnp.bfloat16), val_blk, preferred_element_type=jnp.float32
        )
        acc = acc * factor[:, :, None] + update
        return (new_top, total, acc)

    def visit(carry, pair, back):
        if back == 0:
            return accumulate(carry, pair, back)
        return accumulate(carry, pair, back)

    carry = (
        jnp.full((heads_dev, rows), -1e30, jnp.float32),
        jnp.zeros((heads_dev, rows), jnp.float32),
        jnp.zeros((heads_dev, rows, HEAD_DIM), jnp.float32),
    )
    own = (keys, mixed)
    moving = own
    for back in range(SPAN):
        if back > 0:
            moving = from_behind((moving[0], moving[1]), "seq", 1)
        carry = visit(carry, moving, back)
    top, total, acc = carry
    output = acc / total[:, :, None]
    attended = jnp.transpose(output, (1, 0, 2)).astype(jnp.bfloat16).reshape(rows, width)
    return (mixed, attended)


def solution(mesh):
    placed = (
        P("seq", "ch"),
        P("ch"),
        P("ch", None),
        P("seq", "ch"),
        P("seq", "ch"),
        P("seq", "ch"),
        P(),
    )
    return jax.shard_map(
        shards,
        mesh=mesh,
        in_specs=placed,
        out_specs=(P("seq", "ch"), P("seq", "ch")),
        check_vma=False,
    )
```

profile of v0, /device:TPU:128, one launch (start us, length us, event | category | flops | bytes accessed | tf_op | source)
XLA Modules:
  0.0 208.9 jit_solution(3769503696999829764)
XLA Ops:
  0.6 0.0 copy-start
  0.6 0.0 copy-start.9
  0.7 0.0 copy-start.10
  0.7 1.6 copy.54
  2.2 0.3 fusion.15
  2.5 2.5 %psum.7 = f32[256]{0:T(256)S(1)} all-reduce(f32[256]{0:T(256)S(1)} %fusion.15), channel_id=1, replica_groups=mesh['seq'=128,'ch'=2] {'ch'}, use_global_device_ids=true, to_apply=%region_1.2 | all-reduce | flops 256 | bytes 2048 | tf_op jit(solution)/shard_map/psum | solution.py:43
  5.0 1.0 fusion.17
  6.1 0.8 slice.24
  6.9 3.4 %collective-permute-start = (bf16[128,2048]{0,1:T(8,128)(2,1)}, bf16[128,2048]{0,1:T(8,128)(2,1)}, u32[]{:S(2)}, u32[]{:S(2)}) collective-permute-start(bf16[128,2048]{0,1:T(8,128)(2,1)} %slice.24), channel_id=1, source_target_pairs={{0,2},{2,4},{4,6},{6,8},{8,10},{10,12},{12,14},{14,16},{16,18},{18... | collective-permute-start | bytes 1572872 | tf_op jit(solution)/shard_map/ppermute | solution.py:14
  10.3 2.3 %copy.64 = bf16[256,2048]{0,1:T(8,128)(2,1)} copy(bf16[256,2048]{1,0:T(8,128)(2,1)} %param.12) | data formatting | bytes 2097152 | tf_op args[5]
  12.5 3.4 %collective-permute-start.1 = (bf16[256,2048]{0,1:T(8,128)(2,1)}, bf16[256,2048]{0,1:T(8,128)(2,1)}, u32[]{:S(2)}, u32[]{:S(2)}) collective-permute-start(bf16[256,2048]{0,1:T(8,128)(2,1)} %copy.64), channel_id=1, source_target_pairs={{0,2},{2,4},{4,6},{6,8},{8,10},{10,12},{12,14},{14,16},{16,18},{18... | collective-permute-start | bytes 3145736 | tf_op jit(solution)/shard_map/ppermute | solution.py:14
  16.0 0.0 copy-done.9
  16.0 0.1 copy.55
  16.1 0.1 reduce-window.9
  16.2 0.1 reduce
  16.3 0.1 select_reduce_fusion
  16.4 0.1 broadcast_compare_fusion
  16.5 0.0 copy-done.10
  16.5 19.9 %select_bitcast_fusion.1 = (bf16[128,128,256]{0,2,1:T(8,128)(2,1)}, bf16[128,128,256]{0,2,1:T(8,128)(2,1)}) fusion(pred[128,256]{1,0:T(8,128)(4,1)S(1)} %get-tuple-element.36, pred[128,256]{1,0:T(8,128)(4,1)S(1)} %get-tuple-element.35, bf16[128,128]{1,0:T(8,128)(2,1)S(1)} %copy-done.10, s32[128,256]{1,0:T(8,128)S(1)} %subtract_add_fusion), kind=kOutput, calls=%fused_computation.3 | convolution fusion | flops 1090519040 | bytes 17006592 | tf_op jit(solution)/shard_map/nml,gl->gnm/dot_general | solution.py:30
  36.5 12.3 %copy.56 = bf16[128,128,256]{2,1,0:T(8,128)(2,1)} copy(bf16[128,128,256]{0,2,1:T(8,128)(2,1)} %get-tuple-element.14) | data formatting | bytes 16777216 | tf_op jit(solution)/shard_map/jit(_where)/select_n | solution.py:56
  48.8 12.5 %copy.58 = bf16[128,128,256]{2,1,0:T(8,128)(2,1)} copy(bf16[128,128,256]{0,2,1:T(8,128)(2,1)} %get-tuple-element.15) | data formatting | bytes 16777216 | tf_op jit(solution)/shard_map/jit(_where)/select_n | solution.py:56
  61.3 5.7 %fusion.95 = f32[128,16,128]{2,1,0:T(8,128)S(1)} fusion(bf16[256,128,16]{0,2,1:T(8,128)(2,1)S(1)} %bitcast.167, bf16[128,128,256]{2,1,0:T(8,128)(2,1)} %copy.58), kind=kOutput, calls=%fused_computation.131 | convolution fusion | flops 134217728 | bytes 10485760 | tf_op jit(solution)/shard_map/gnm,mgc->ngc/dot_general | solution.py:57
  66.9 1.3 copy.59
  68.2 0.0 collective-permute-done
  68.3 1.2 pad_maximum_fusion
  69.4 0.0 copy-start.6
  69.4 5.7 %fusion.94 = f32[128,16,128]{2,1,0:T(8,128)S(1)} fusion(bf16[256,128,16]{0,2,1:T(8,128)(2,1)S(1)} %bitcast.168, bf16[128,128,256]{2,1,0:T(8,128)(2,1)} %copy.56), kind=kOutput, calls=%fused_computation.130 | convolution fusion | flops 134217728 | bytes 10485760 | tf_op jit(solution)/shard_map/gnm,mgc->ngc/dot_general | solution.py:57
  75.2 1.3 copy.57
  76.5 0.0 copy-done.6
  76.5 1.8 multiply_convert_fusion.1
  78.3 0.1 pad_maximum_fusion.1
  78.4 0.0 copy-start.5
  78.4 3.1 %collective-permute-start.2 = (bf16[256,2048]{1,0:T(8,128)(2,1)S(1)}, bf16[256,2048]{1,0:T(8,128)(2,1)}, u32[]{:S(2)}, u32[]{:S(2)}) collective-permute-start(bf16[256,2048]{1,0:T(8,128)(2,1)S(1)} %pad_maximum_fusion.1), channel_id=1, source_target_pairs={{0,2},{2,4},{4,6},{6,8},{8,10},{10,12},{12,14},{14,16},{16,18},{18... | collective-permute-start | bytes 3145736 | tf_op jit(solution)/shard_map/ppermute | solution.py:14
  81.5 0.0 collective-permute-done.1
  81.5 3.4 %collective-permute-start.3 = (bf16[256,2048]{0,1:T(8,128)(2,1)}, bf16[256,2048]{0,1:T(8,128)(2,1)S(1)}, u32[]{:S(2)}, u32[]{:S(2)}) collective-permute-start(bf16[256,2048]{0,1:T(8,128)(2,1)} %collective-permute-done.1), channel_id=1, source_target_pairs={{0,2},{2,4},{4,6},{6,8},{8,10},{10,12},{12,14},{14,16},{16,18},{18... | collective-permute-start | bytes 3145736 | tf_op jit(solution)/shard_map/ppermute | solution.py:14
  85.0 0.3 compare_and_fusion.3
  85.3 26.7 %collective-permute-done.2 = bf16[256,2048]{1,0:T(8,128)(2,1)} collective-permute-done((bf16[256,2048]{1,0:T(8,128)(2,1)S(1)}, bf16[256,2048]{1,0:T(8,128)(2,1)}, u32[]{:S(2)}, u32[]{:S(2)}) %collective-permute-start.2) | collective-permute-done | bytes 1048608 | tf_op jit(solution)/shard_map/ppermute | solution.py:14
  111.9 1.9 collective-permute-start.4
  113.8 20.4 %collective-permute-done.3 = bf16[256,2048]{0,1:T(8,128)(2,1)S(1)} collective-permute-done((bf16[256,2048]{0,1:T(8,128)(2,1)}, bf16[256,2048]{0,1:T(8,128)(2,1)S(1)}, u32[]{:S(2)}, u32[]{:S(2)}) %collective-permute-start.3) | collective-permute-done | bytes 1048608 | tf_op jit(solution)/shard_map/ppermute | solution.py:14
  134.3 1.9 collective-permute-start.5
  136.2 0.0 copy-done
  136.2 4.0 %fusion.3 = (f32[16,256]{1,0:T(8,128)S(1)}, f32[16,256,256]{1,2,0:T(8,128)}) fusion(pred[256,256]{0,1:T(8,128)(4,1)S(1)} %get-tuple-element.21, bf16[256,2048]{1,0:T(8,128)(2,1)} %param.12, bf16[256,2048]{1,0:T(8,128)(2,1)S(1)} %copy-done), kind=kOutput, calls=%fused_computation.14 | convolution fusion | flops 271577088 | bytes 6373376 | tf_op jit(solution)/shard_map/rhd,khd->hrk/dot_general | solution.py:76
  140.3 1.3 copy.62
  141.6 4.1 %fusion.4 = (f32[16,256]{1,0:T(8,128)S(1)}, f32[16,256,256]{1,2,0:T(8,128)}) fusion(pred[256,256]{0,1:T(8,128)(4,1)S(1)} %get-tuple-element.22, bf16[256,16,128]{0,2,1:T(8,128)(2,1)} %bitcast.13, bf16[256,2048]{1,0:T(8,128)(2,1)S(1)} %copy-done), kind=kOutput, calls=%fused_computation.15 | convolution fusion | flops 271577088 | bytes 6373376 | tf_op jit(solution)/shard_map/rhd,khd->hrk/dot_general | solution.py:76
  145.7 1.5 copy.67
  147.2 2.9 %fusion.5 = (f32[16,256]{1,0:T(8,128)S(1)}, f32[16,256,256]{1,2,0:T(8,128)}) fusion(pred[256,256]{0,1:T(8,128)(4,1)S(1)} %get-tuple-element.23, bf16[256,16,128]{0,2,1:T(8,128)(2,1)S(1)} %bitcast.171, bf16[256,2048]{1,0:T(8,128)(2,1)S(1)} %copy-done), kind=kOutput, calls=%fused_computation.16 | convolution fusion | flops 271577088 | bytes 6373376 | tf_op jit(solution)/shard_map/rhd,khd->hrk/dot_general | solution.py:76
  150.1 6.8 %collective-permute-done.4 = bf16[256,2048]{1,0:T(8,128)(2,1)} collective-permute-done((bf16[256,2048]{1,0:T(8,128)(2,1)}, bf16[256,2048]{1,0:T(8,128)(2,1)}, u32[]{:S(2)}, u32[]{:S(2)}) %collective-permute-start.4) | collective-permute-done | bytes 1048608 | tf_op jit(solution)/shard_map/ppermute | solution.py:14
  156.9 2.3 %copy.71 = bf16[256,2048]{0,1:T(8,128)(2,1)} copy(bf16[256,2048]{1,0:T(8,128)(2,1)} %collective-permute-done.4) | data formatting | bytes 2097152 | tf_op jit(solution)/shard_map/ppermute | solution.py:14
  159.1 2.5 %collective-permute-start.6 = (bf16[256,2048]{1,0:T(8,128)(2,1)}, bf16[256,2048]{1,0:T(8,128)(2,1)}, u32[]{:S(2)}, u32[]{:S(2)}) collective-permute-start(bf16[256,2048]{1,0:T(8,128)(2,1)} %collective-permute-done.4), channel_id=1, source_target_pairs={{0,2},{2,4},{4,6},{6,8},{8,10},{10,12},{12,14},{14,16},{16,18},{18... | collective-permute-start | bytes 3145736 | tf_op jit(solution)/shard_map/ppermute | solution.py:14
  161.6 17.7 %collective-permute-done.5 = bf16[256,2048]{0,1:T(8,128)(2,1)} collective-permute-done((bf16[256,2048]{0,1:T(8,128)(2,1)S(1)}, bf16[256,2048]{0,1:T(8,128)(2,1)}, u32[]{:S(2)}, u32[]{:S(2)}) %collective-permute-start.5) | collective-permute-done | bytes 1048608 | tf_op jit(solution)/shard_map/ppermute | solution.py:14
  179.3 2.2 %fusion.6 = (f32[16,256]{1,0:T(8,128)S(1)}, f32[16,256,256]{1,2,0:T(8,128)S(1)}) fusion(pred[256,256]{0,1:T(8,128)(4,1)S(1)} %get-tuple-element.24, bf16[256,16,128]{0,2,1:T(8,128)(2,1)} %bitcast.21, bf16[256,2048]{1,0:T(8,128)(2,1)S(1)} %copy-done), kind=kOutput, calls=%fused_computation.17 | convolution fusion | flops 271577088 | bytes 6373376 | tf_op jit(solution)/shard_map/rhd,khd->hrk/dot_general | solution.py:76
  181.6 0.0 copy-done.3
  181.6 0.0 copy-done.8
  181.6 2.7 %fusion.20 = f32[16,256,128]{1,2,0:T(8,128)} fusion(bf16[256,16,128]{0,2,1:T(8,128)(2,1)S(1)} %bitcast.174, f32[16,256,256]{1,2,0:T(8,128)S(1)} %copy-done.3, f32[16,256]{1,0:T(8,128)S(1)} %get-tuple-element.12, pred[256,256]{0,1:T(8,128)(4,1)S(1)} %get-tuple-element.23), kind=kOutput, calls=%fused_computation.32 | convolution fusion | flops 273678336 | bytes 7421952 | tf_op jit(solution)/shard_map/hrk,khd->hrd/dot_general | solution.py:83
  184.2 2.2 %fusion.11 = (f32[16,256]{1,0:T(8,128)S(1)}, f32[16,256]{1,0:T(8,128)S(1)}) fusion(f32[16,256,256]{1,2,0:T(8,128)S(1)} %copy-done.3, f32[16,256]{1,0:T(8,128)S(1)} %get-tuple-element.12, pred[256,256]{0,1:T(8,128)(4,1)S(1)} %get-tuple-element.23, f32[16,256]{1,0:T(8,128)S(1)} %get-tuple-element.11, f32[16,256,256]{1,2,0:T(8,128)S(1)} %get-tuple-element.28, ...), kind=kLoop, calls=%fused_computation.22 | loop fusion | flops 10477568 | bytes 8585216 | tf_op jit(solution)/shard_map/reduce_sum | solution.py:82
  186.5 1.2 copy-done.4
  187.7 2.2 %fusion.7 = (f32[16,256]{1,0:T(8,128)S(1)}, f32[16,256]{1,0:T(8,128)S(1)}) fusion(f32[16,256,256]{1,2,0:T(8,128)S(1)} %copy-done.4, f32[16,256]{1,0:T(8,128)S(1)} %get-tuple-element.20, pred[256,256]{0,1:T(8,128)(4,1)S(1)} %get-tuple-element.21, f32[16,256]{1,0:T(8,128)S(1)} %get-tuple-element.13, f32[16,256,256]{1,2,0:T(8,128)S(1)} %copy-done.1, ...), kind=kLoop, calls=%fused_computation.18 | loop fusion | flops 10477568 | bytes 8585216 | tf_op jit(solution)/shard_map/reduce_sum | solution.py:82
  190.0 0.0 copy-start.7
  190.0 2.5 %fusion.22 = f32[16,256,128]{1,2,0:T(8,128)} fusion(bf16[256,16,128]{0,2,1:T(8,128)(2,1)S(1)} %bitcast.173, f32[16,256,256]{1,2,0:T(8,128)S(1)} %copy-done.1, f32[16,256]{1,0:T(8,128)S(1)} %get-tuple-element.13, pred[256,256]{0,1:T(8,128)(4,1)S(1)} %get-tuple-element.22), kind=kOutput, calls=%fused_computation.33 | convolution fusion | flops 273678336 | bytes 7421952 | tf_op jit(solution)/shard_map/hrk,khd->hrd/dot_general | solution.py:83
  192.5 2.5 %fusion.24 = f32[16,256,128]{1,2,0:T(8,128)} fusion(bf16[256,16,128]{0,2,1:T(8,128)(2,1)S(1)} %bitcast.172, f32[16,256,256]{1,2,0:T(8,128)S(1)} %copy-done.4, f32[16,256]{1,0:T(8,128)S(1)} %get-tuple-element.20, pred[256,256]{0,1:T(8,128)(4,1)S(1)} %get-tuple-element.21), kind=kOutput, calls=%fused_computation.34 | convolution fusion | flops 273678336 | bytes 7421952 | tf_op jit(solution)/shard_map/hrk,khd->hrd/dot_general | solution.py:83
  195.0 5.4 %collective-permute-done.6 = bf16[256,2048]{1,0:T(8,128)(2,1)} collective-permute-done((bf16[256,2048]{1,0:T(8,128)(2,1)}, bf16[256,2048]{1,0:T(8,128)(2,1)}, u32[]{:S(2)}, u32[]{:S(2)}) %collective-permute-start.6) | collective-permute-done | bytes 1048608 | tf_op jit(solution)/shard_map/ppermute | solution.py:14
  200.4 1.5 copy.75
  201.9 5.6 %fusion.27 = bf16[256,16,128]{0,2,1:T(8,128)(2,1)S(1)} fusion(f32[16,256,128]{1,2,0:T(8,128)} %fusion.20, f32[16,256,128]{1,2,0:T(8,128)} %fusion.22, f32[16,256,128]{1,2,0:T(8,128)} %fusion.24, f32[256,16]{0,1:T(8,128)S(1)} %get-tuple-element.8, f32[256,16]{0,1:T(8,128)S(1)} %get-tuple-element.10, f32[256,16]{0,1:T(8,128)S(1)} %get-tuple-element.9, ...), kind=kOutput, calls=%fused_computation.37 | convolution fusion | flops 278396928 | bytes 12746752 | tf_op jit(solution)/shard_map/hrk,khd->hrd/dot_general | solution.py:83
  207.5 1.4 copy.77
  (20 shorter events, 0.1 us)
Async XLA Ops:
  0.6 135.6 %copy-start = (bf16[256,2048]{1,0:T(8,128)(2,1)S(1)}, bf16[256,2048]{1,0:T(8,128)(2,1)}, u32[]{:S(2)}) copy-start(bf16[256,2048]{1,0:T(8,128)(2,1)} %param.11) | copy-start | bytes 3145732
  0.6 15.3 %copy-start.9 = (s32[48]{0:T(128)S(1)}, s32[48]{0:T(128)}, u32[]{:S(2)}) copy-start(s32[48]{0:T(128)} %param.13) | copy-start | bytes 580
  0.7 15.9 %copy-start.10 = (bf16[128,128]{1,0:T(8,128)(2,1)S(1)}, bf16[128,128]{1,0:T(8,128)(2,1)}, u32[]{:S(2)}) copy-start(bf16[128,128]{1,0:T(8,128)(2,1)} %param.9) | copy-start | bytes 98308
  6.9 61.4 %collective-permute-start = (bf16[128,2048]{0,1:T(8,128)(2,1)}, bf16[128,2048]{0,1:T(8,128)(2,1)}, u32[]{:S(2)}, u32[]{:S(2)}) collective-permute-start(bf16[128,2048]{0,1:T(8,128)(2,1)} %slice.24), channel_id=1, source_target_pairs={{0,2},{2,4},{4,6},{6,8},{8,10},{10,12},{12,14},{14,16},{16,18},{18... | collective-permute-start | bytes 1572872 | tf_op jit(solution)/shard_map/ppermute | solution.py:14
  12.5 69.0 %collective-permute-start.1 = (bf16[256,2048]{0,1:T(8,128)(2,1)}, bf16[256,2048]{0,1:T(8,128)(2,1)}, u32[]{:S(2)}, u32[]{:S(2)}) collective-permute-start(bf16[256,2048]{0,1:T(8,128)(2,1)} %copy.64), channel_id=1, source_target_pairs={{0,2},{2,4},{4,6},{6,8},{8,10},{10,12},{12,14},{14,16},{16,18},{18... | collective-permute-start | bytes 3145736 | tf_op jit(solution)/shard_map/ppermute | solution.py:14
  69.4 7.1 %copy-start.6 = (f32[128,2048]{1,0:T(8,128)S(1)}, f32[128,2048]{1,0:T(8,128)}, u32[]{:S(2)}) copy-start(f32[128,2048]{1,0:T(8,128)} %copy.59) | copy-start | bytes 3145732
  78.4 63.2 %copy-start.5 = (bf16[256,2048]{1,0:T(8,128)(2,1)}, bf16[256,2048]{1,0:T(8,128)(2,1)S(1)}, u32[]{:S(2)}) copy-start(bf16[256,2048]{1,0:T(8,128)(2,1)S(1)} %pad_maximum_fusion.1) | copy-start | bytes 3145732
  78.4 33.5 %collective-permute-start.2 = (bf16[256,2048]{1,0:T(8,128)(2,1)S(1)}, bf16[256,2048]{1,0:T(8,128)(2,1)}, u32[]{:S(2)}, u32[]{:S(2)}) collective-permute-start(bf16[256,2048]{1,0:T(8,128)(2,1)S(1)} %pad_maximum_fusion.1), channel_id=1, source_target_pairs={{0,2},{2,4},{4,6},{6,8},{8,10},{10,12},{12,14},{14,16},{16,18},{18... | collective-permute-start | bytes 3145736 | tf_op jit(solution)/shard_map/ppermute | solution.py:14
  81.5 52.8 %collective-permute-start.3 = (bf16[256,2048]{0,1:T(8,128)(2,1)}, bf16[256,2048]{0,1:T(8,128)(2,1)S(1)}, u32[]{:S(2)}, u32[]{:S(2)}) collective-permute-start(bf16[256,2048]{0,1:T(8,128)(2,1)} %collective-permute-done.1), channel_id=1, source_target_pairs={{0,2},{2,4},{4,6},{6,8},{8,10},{10,12},{12,14},{14,16},{16,18},{18... | collective-permute-start | bytes 3145736 | tf_op jit(solution)/shard_map/ppermute | solution.py:14
  111.9 44.9 %collective-permute-start.4 = (bf16[256,2048]{1,0:T(8,128)(2,1)}, bf16[256,2048]{1,0:T(8,128)(2,1)}, u32[]{:S(2)}, u32[]{:S(2)}) collective-permute-start(bf16[256,2048]{1,0:T(8,128)(2,1)} %collective-permute-done.2), channel_id=1, source_target_pairs={{0,2},{2,4},{4,6},{6,8},{8,10},{10,12},{12,14},{14,16},{16,18},{18... | collective-permute-start | bytes 3145736 | tf_op jit(solution)/shard_map/ppermute | solution.py:14
  134.3 45.0 %collective-permute-start.5 = (bf16[256,2048]{0,1:T(8,128)(2,1)S(1)}, bf16[256,2048]{0,1:T(8,128)(2,1)}, u32[]{:S(2)}, u32[]{:S(2)}) collective-permute-start(bf16[256,2048]{0,1:T(8,128)(2,1)S(1)} %collective-permute-done.3), channel_id=1, source_target_pairs={{0,2},{2,4},{4,6},{6,8},{8,10},{10,12},{12,14},{14,16},{16,18},{18... | collective-permute-start | bytes 3145736 | tf_op jit(solution)/shard_map/ppermute | solution.py:14
  159.1 22.4 %copy-start.3 = (f32[16,256,256]{1,2,0:T(8,128)S(1)}, f32[16,256,256]{1,2,0:T(8,128)}, u32[]{:S(2)}) copy-start(f32[16,256,256]{1,2,0:T(8,128)} %get-tuple-element.30) | copy-start | bytes 12582916
  159.1 22.4 %copy-start.8 = (bf16[256,2048]{0,1:T(8,128)(2,1)S(1)}, bf16[256,2048]{0,1:T(8,128)(2,1)}, u32[]{:S(2)}) copy-start(bf16[256,2048]{0,1:T(8,128)(2,1)} %copy.71) | copy-start | bytes 3145732
  159.1 41.3 %collective-permute-start.6 = (bf16[256,2048]{1,0:T(8,128)(2,1)}, bf16[256,2048]{1,0:T(8,128)(2,1)}, u32[]{:S(2)}, u32[]{:S(2)}) collective-permute-start(bf16[256,2048]{1,0:T(8,128)(2,1)} %collective-permute-done.4), channel_id=1, source_target_pairs={{0,2},{2,4},{4,6},{6,8},{8,10},{10,12},{12,14},{14,16},{16,18},{18... | collective-permute-start | bytes 3145736 | tf_op jit(solution)/shard_map/ppermute | solution.py:14
  181.5 2.7 %copy-start.2 = (f32[16,256,256]{1,2,0:T(8,128)}, f32[16,256,256]{1,2,0:T(8,128)S(1)}, u32[]{:S(2)}) copy-start(f32[16,256,256]{1,2,0:T(8,128)S(1)} %get-tuple-element.28) | copy-start | bytes 12582916
  184.2 2.2 %copy-start.1 = (f32[16,256,256]{1,2,0:T(8,128)S(1)}, f32[16,256,256]{1,2,0:T(8,128)}, u32[]{:S(2)}) copy-start(f32[16,256,256]{1,2,0:T(8,128)} %get-tuple-element.32) | copy-start | bytes 12582916
  184.2 3.5 %copy-start.4 = (f32[16,256,256]{1,2,0:T(8,128)S(1)}, f32[16,256,256]{1,2,0:T(8,128)}, u32[]{:S(2)}) copy-start(f32[16,256,256]{1,2,0:T(8,128)} %get-tuple-element.34) | copy-start | bytes 12582916
  190.0 2.6 %copy-start.7 = (bf16[256,2048]{0,1:T(8,128)(2,1)S(1)}, bf16[256,2048]{0,1:T(8,128)(2,1)}, u32[]{:S(2)}) copy-start(bf16[256,2048]{0,1:T(8,128)(2,1)} %copy.62) | copy-start | bytes 3145732
where the time goes:
time: 210 us; the launch traced here: 209 us
  waiting for transfers between devices  77 us (37%)
  matrix products  57.9 us (28%)
  local copies, waits for them, and re-layouts  41.4 us (20%)
  starting transfers between devices  19.6 us (9%)
  other arithmetic  9.58 us (5%)
  blocking collectives  2.46 us (1%)
    ppermute x7, waiting for transfers between devices, from_behind(): lax.ppermute(value, axis, [(source, source + steps) for source in range(i...  77 us
    select_n x2, local copies, waits for them, and re-layouts, shards(): matrix = jnp.where(inside[None], banded, jnp.zeros_like(banded))  24.8 us
    dot_general x1, matrix products, band_taps(): jnp.einsum('nml,gl->gnm', onehot, filters, preferred_element_type=jnp.flo...  19.9 us
    ppermute x7, starting transfers between devices, from_behind(): lax.ppermute(value, axis, [(source, source + steps) for source in range(i...  19.6 us
    dot_general x4, matrix products, accumulate(): jnp.einsum('hrk,khd->hrd', weight.astype(jnp.bfloat16), val_blk, preferre...  13.3 us
    dot_general x4, matrix products, accumulate(): jnp.einsum('rhd,khd->hrk', query, key_blk, preferred_element_type=jnp.flo...  13.3 us
    dot_general x2, matrix products, shards(): jnp.einsum('gnm,mgc->ngc', matrix, src_rows.reshape(2 * taps_count, group...  11.4 us
    unnamed x25, local copies, waits for them, and re-layouts  6.52 us
  transfers between devices with their start and end apart: 7, of which 5 were waited for; matrix products, arithmetic and copies ran while one was open for 46% of the time, Pallas kernels for 0%

commit v1 on v0

v1 whole, which is shorter than its diff:
```python
import jax
import jax.numpy as jnp
from jax import lax
from jax.experimental import pallas as pl
from jax.experimental.pallas import tpu as pltpu
from jax.sharding import PartitionSpec as P

HEAD_DIM = 128
GROUP = 16
TAPS = 128
CONV_CH = 4096
RING = 4
VMEM_LIMIT = 48 * 1024 * 1024
ANY = pl.BlockSpec(memory_space=pl.ANY)
SMEM = pl.BlockSpec(memory_space=pltpu.SMEM)
VMEM = pl.BlockSpec(memory_space=pltpu.VMEM)
NEG = -1e30


def begin_of(doc_lengths, positions):
    ends = jnp.cumsum(doc_lengths)
    starts = ends - doc_lengths
    inside = starts[None, :] <= positions[:, None]
    return jnp.max(jnp.where(inside, starts[None, :], 0), axis=1)


def params():
    return pltpu.CompilerParams(vmem_limit_bytes=VMEM_LIMIT)


def cost(flops, nbytes, trans=0):
    return pl.CostEstimate(flops=flops, bytes_accessed=nbytes, transcendentals=trans)


def quarters(place, *arrays):
    rows, width = arrays[0].shape
    part = width // RING
    count = len(arrays)

    def kernel(place_ref, *refs):
        ins, outs, sem = refs[:count], refs[count : count + count * RING], refs[-1]
        place = place_ref[0]
        copies = []
        for a in range(count):
            for d in range(RING):
                low = pl.multiple_of(lax.rem(place + d, RING) * part, part)
                copies.append(
                    pltpu.make_async_copy(
                        ins[a].at[:, pl.ds(low, part)], outs[a * RING + d], sem.at[a * RING + d]
                    )
                )
        for copy in copies:
            copy.start()
        for copy in copies:
            copy.wait()

    out = pl.pallas_call(
        kernel,
        out_shape=[
            jax.ShapeDtypeStruct((rows, part), arrays[0].dtype) for _ in range(count * RING)
        ],
        in_specs=[SMEM] + [ANY] * count,
        out_specs=[ANY] * (count * RING),
        scratch_shapes=[pltpu.SemaphoreType.DMA((count * RING,))],
        compiler_params=params(),
        cost_estimate=cost(0, 4 * count * rows * width),
        name="quarters",
    )(place, *arrays)
    return [out[a * RING : (a + 1) * RING] for a in range(count)]


def whole_width(place, pieces):
    rows, part = pieces[0].shape

    def kernel(place_ref, *refs):
        ins, out, sem = refs[:RING], refs[RING], refs[-1]
        place = place_ref[0]
        copies = []
        for d in range(RING):
            low = pl.multiple_of(lax.rem(place + RING - d, RING) * part, part)
            copies.append(
                pltpu.make_async_copy(ins[d], out.at[:, pl.ds(low, part)], sem.at[d])
            )
        for copy in copies:
            copy.start()
        for copy in copies:
            copy.wait()

    return pl.pallas_call(
        kernel,
        out_shape=jax.ShapeDtypeStruct((rows, part * RING), pieces[0].dtype),
        in_specs=[SMEM] + [ANY] * RING,
        out_specs=ANY,
        scratch_shapes=[pltpu.SemaphoreType.DMA((RING,))],
        compiler_params=params(),
        cost_estimate=cost(0, 4 * rows * part * RING),
        name="whole_width",
    )(place, *pieces)


def last_shards(place, pieces):
    rows, part = pieces[0].shape

    def kernel(place_ref, *refs):
        ins, out, sem = refs[:RING], refs[RING], refs[-1]
        place = place_ref[0]

        def copy_of(d):
            shard = lax.rem(place + RING - d, RING)
            low = pl.multiple_of(jnp.maximum(shard - 1, 0) * rows, rows)
            return shard, pltpu.make_async_copy(ins[d], out.at[pl.ds(low, rows), :], sem.at[d])

        for d in range(RING):
            shard, copy = copy_of(d)
            pl.when(shard > 0)(copy.start)
        for d in range(RING):
            shard, copy = copy_of(d)
            pl.when(shard > 0)(copy.wait)

    return pl.pallas_call(
        kernel,
        out_shape=jax.ShapeDtypeStruct((rows * (RING - 1), part), pieces[0].dtype),
        in_specs=[SMEM] + [ANY] * RING,
        out_specs=ANY,
        scratch_shapes=[pltpu.SemaphoreType.DMA((RING,))],
        compiler_params=params(),
        cost_estimate=cost(0, 3 * rows * part * RING),
        name="last_shards",
    )(place, *pieces)


def convolve(place, conv_in, tail, rms, gain, taps, gate, begin):
    rows, width = conv_in.shape
    part = width // RING
    lanes = 128
    per = lanes // GROUP
    blocks = rows // TAPS

    def kernel(place_ref, x_ref, tail_ref, rms_ref, gain_ref, taps_ref, gate_ref, begin_ref, *refs):
        mixed_ref, outs = refs[0], refs[1 : 1 + RING]
        masks, src, lhs = refs[1 + RING :]
        place = place_ref[0]
        out_row = lax.broadcasted_iota(jnp.int32, (TAPS, lanes), 0)
        src_col = lax.broadcasted_iota(jnp.int32, (TAPS, lanes), 1)
        for b in range(blocks):
            first = begin_ref[b * TAPS : (b + 1) * TAPS, :]
            low = b * TAPS
            before = (src_col > out_row) & (src_col + (low - TAPS) >= first)
            inside = (src_col <= out_row) & (src_col + low >= first)
            masks[2 * b] = jnp.where(before, 1.0, 0.0).astype(jnp.bfloat16)
            masks[2 * b + 1] = jnp.where(inside, 1.0, 0.0).astype(jnp.bfloat16)
        lane_group = lax.broadcasted_iota(jnp.int32, (TAPS, lanes), 1) // GROUP

        def chunk(d, c):
            at = lax.rem(place + d, RING) * (part // lanes) + c
            low = pl.multiple_of(at * lanes, lanes)
            cols = pl.ds(low, lanes)
            src[:TAPS, :] = tail_ref[:, cols]
            src[TAPS:, :] = (
                x_ref[:, cols].astype(jnp.float32) * rms_ref[...] * gain_ref[:, cols]
            ).astype(jnp.bfloat16)
            rows8 = taps_ref[pl.ds(pl.multiple_of(at * per, per), per), :]
            for j in range(per):
                line = jnp.broadcast_to(rows8[j : j + 1, :], (TAPS, lanes))
                band = pltpu.roll(line, 1, 1, stride=1, stride_axis=0).astype(jnp.bfloat16)
                for b in range(blocks):
                    at_rows = pl.ds(j * TAPS, TAPS)
                    lhs[b, at_rows, :lanes] = band * masks[2 * b]
                    lhs[b, at_rows, lanes:] = band * masks[2 * b + 1]
            for b in range(blocks):
                full = jnp.dot(
                    lhs[b],
                    src[b * TAPS : (b + 2) * TAPS, :],
                    preferred_element_type=jnp.float32,
                )
                picked = full[:TAPS]
                for j in range(1, per):
                    picked = jnp.where(lane_group == j, full[j * TAPS : (j + 1) * TAPS], picked)
                at_rows = pl.ds(b * TAPS, TAPS)
                out = (gate_ref[at_rows, cols].astype(jnp.float32) * picked).astype(jnp.bfloat16)
                mixed_ref[at_rows, cols] = out
                outs[d][at_rows, c * lanes : (c + 1) * lanes] = out

        for d in (2, 1, 3, 0):
            for c in range(part // lanes):
                chunk(d, c)

    out = pl.pallas_call(
        kernel,
        out_shape=[jax.ShapeDtypeStruct((rows, width), jnp.bfloat16)]
        + [jax.ShapeDtypeStruct((rows, part), jnp.bfloat16) for _ in range(RING)],
        in_specs=[SMEM] + [VMEM] * 7,
        out_specs=[VMEM] * (1 + RING),
        scratch_shapes=[
            pltpu.VMEM((2 * blocks, TAPS, lanes), jnp.bfloat16),
            pltpu.VMEM((rows + TAPS, lanes), jnp.bfloat16),
            pltpu.VMEM((blocks, per * TAPS, 2 * lanes), jnp.bfloat16),
        ],
        compiler_params=params(),
        cost_estimate=cost(2 * rows * 2 * TAPS * width * per, 10 * rows * width),
        name="convolve",
    )(place, conv_in, tail, rms, gain, taps, gate, begin)
    return out[0], list(out[1:])


def attend(place, begin, queries, keys, values, key_halo, value_halo):
    rows, part = queries[0].shape
    heads = part // HEAD_DIM
    back = (RING - 1) * rows
    span = RING * rows
    scale = HEAD_DIM**-0.5 * 1.4426950408889634

    def kernel(place_ref, begin_ref, *refs):
        q_in, k_in, v_in = refs[:RING], refs[RING : 2 * RING], refs[2 * RING : 3 * RING]
        kh_in, vh_in = refs[3 * RING : 3 * RING + 2]
        outs = refs[3 * RING + 2 : 4 * RING + 2]
        q_all, k_all, v_all, o_all, bias, sem, out_sem = refs[4 * RING + 2 :]
        place = place_ref[0]
        copies = []

        def fetch(source, target):
            copies.append(pltpu.make_async_copy(source, target, sem.at[len(copies)]))

        for d in range(RING):
            low = pl.multiple_of(lax.rem(place + RING - d, RING) * rows, rows)
            fetch(q_in[d], q_all.at[pl.ds(low, rows), :])
            fetch(k_in[d], k_all.at[pl.ds(back + low, rows), :])
            fetch(v_in[d], v_all.at[pl.ds(back + low, rows), :])
        fetch(kh_in, k_all.at[pl.ds(0, back), :])
        fetch(vh_in, v_all.at[pl.ds(0, back), :])
        for copy in copies:
            copy.start()
        for copy in copies:
            copy.wait()
        row = lax.broadcasted_iota(jnp.int32, (rows, 128), 0)
        col = lax.broadcasted_iota(jnp.int32, (rows, 128), 1)

        def shard(s, _):
            low = pl.multiple_of(s * rows, rows)
            first = begin_ref[pl.ds(low, rows), :] - low
            for c in range(span // 128):
                key = col + c * 128
                valid = key >= first
                if (c + 1) * 128 > back:
                    valid = valid & (key <= row + back)
                bias[:, c * 128 : (c + 1) * 128] = jnp.where(valid, 0.0, NEG)
            for h in range(heads):
                cols = slice(h * HEAD_DIM, (h + 1) * HEAD_DIM)
                score = lax.dot_general(
                    q_all[pl.ds(low, rows), cols],
                    k_all[pl.ds(low, span), cols],
                    (((1,), (1,)), ((), ())),
                    preferred_element_type=jnp.float32,
                )
                score = score + bias[...]
                top = jnp.max(score, axis=1, keepdims=True)
                weight = jnp.exp2((score - top) * scale)
                total = jnp.sum(weight, axis=1, keepdims=True)
                acc = jnp.dot(
                    weight.astype(jnp.bfloat16),
                    v_all[pl.ds(low, span), cols],
                    preferred_element_type=jnp.float32,
                )
                o_all[pl.ds(low, rows), cols] = (acc / total).astype(jnp.bfloat16)
            return 0

        lax.fori_loop(0, RING, shard, 0)
        sends = []
        for d in range(RING):
            low = pl.multiple_of(lax.rem(place + d, RING) * rows, rows)
            sends.append(
                pltpu.make_async_copy(o_all.at[pl.ds(low, rows), :], outs[d], out_sem.at[d])
            )
        for send in sends:
            send.start()
        for send in sends:
            send.wait()

    return pl.pallas_call(
        kernel,
        out_shape=[jax.ShapeDtypeStruct((rows, part), jnp.bfloat16) for _ in range(RING)],
        in_specs=[SMEM, VMEM] + [ANY] * (3 * RING + 2),
        out_specs=[ANY] * RING,
        scratch_shapes=[
            pltpu.VMEM((span, part), jnp.bfloat16),
            pltpu.VMEM((back + span, part), jnp.bfloat16),
            pltpu.VMEM((back + span, part), jnp.bfloat16),
            pltpu.VMEM((span, part), jnp.bfloat16),
            pltpu.VMEM((rows, span), jnp.float32),
            pltpu.SemaphoreType.DMA((3 * RING + 2,)),
            pltpu.SemaphoreType.DMA((RING,)),
        ],
        compiler_params=params(),
        cost_estimate=cost(
            16 * RING * heads * rows * span * HEAD_DIM, 16 * rows * part * RING, heads * span * span
        ),
        name="attend",
    )(place, begin, *queries, *keys, *values, key_halo, value_halo)


def shards(conv_in, norm_gain, filters, gate, queries, keys, doc_lengths):
    rows, width = conv_in.shape
    count = lax.axis_size("seq")
    index = lax.axis_index("seq")
    base = index * rows
    place = lax.rem(index, RING)
    ring_base = (index - place) * rows
    place = place.reshape(1)

    def ring_perm(value, step):
        pairs = [
            (r + i, r + (i + step) % RING) for r in range(0, count, RING) for i in range(RING)
        ]
        return lax.ppermute(value, "seq", pairs)

    def exchange(pieces):
        return [pieces[0]] + [ring_perm(pieces[d], d) for d in range(1, RING)]

    def ahead(value, step):
        return lax.ppermute(value, "seq", [(i, i + step) for i in range(count - step)])

    (query_out, key_out) = quarters(place, queries, keys)
    key_in = exchange(key_out)

    wide = conv_in.astype(jnp.float32)
    energy = lax.psum(jnp.sum(wide * wide, axis=1), "ch")
    rms = lax.rsqrt(energy / CONV_CH + 1e-06)
    rms_wide = jnp.broadcast_to(rms[:, None], (rows, 128))
    last = (
        conv_in[rows - TAPS :].astype(jnp.float32)
        * rms[rows - TAPS :, None]
        * norm_gain[None, :]
    ).astype(jnp.bfloat16)
    tail = ahead(last, 1)

    positions = ring_base + jnp.arange(rows * RING, dtype=jnp.int32)
    begin_ring = begin_of(doc_lengths, positions)
    begin_att = jnp.broadcast_to(
        (begin_ring - ring_base + (RING - 1) * rows)[:, None], (rows * RING, 128)
    )
    begin_own = begin_of(doc_lengths, base + jnp.arange(rows, dtype=jnp.int32)) - base
    begin_conv = jnp.broadcast_to(begin_own[:, None], (rows, 128))

    taps = filters[:, ::-1].astype(jnp.float32)
    mixed, value_out = convolve(
        place, conv_in, tail, rms_wide, norm_gain[None, :], taps, gate, begin_conv
    )
    query_in = exchange(query_out)
    value_in = exchange(value_out)
    key_halo = ahead(last_shards(place, key_in), RING)
    value_halo = ahead(last_shards(place, value_in), RING)
    pieces = attend(place, begin_att, query_in, key_in, value_in, key_halo, value_halo)
    attended = whole_width(place, exchange(pieces))
    return (mixed, attended)


def solution(mesh):
    placed = (
        P("seq", "ch"),
        P("ch"),
        P("ch", None),
        P("seq", "ch"),
        P("seq", "ch"),
        P("seq", "ch"),
        P(),
    )
    return jax.shard_map(
        shards,
        mesh=mesh,
        in_specs=placed,
        out_specs=(P("seq", "ch"), P("seq", "ch")),
        check_vma=False,
    )
```

time: 210 us -> 107 us (0.51)
  matrix products: 57.9 us -> 0 us
  local copies, waits for them, and re-layouts: 41.4 us -> 5.6 us
  waiting for transfers between devices: 77 us -> 49.6 us
  Pallas kernels: 0 us -> 18.9 us
  other arithmetic: 9.58 us -> 3.77 us
  starting transfers between devices: 19.6 us -> 25.1 us
    dot_general x11 -> x0, matrix products: 57.9 us -> none  [the longest x1 19.9 us: band_taps(): jnp.einsum('nml,gl->gnm', onehot, filters, preferred_element_type=jnp.flo...]
    ppermute x7 -> x15, waiting for transfers between devices: 77 us -> 49.6 us  [the longest x12 29.5 us: ring_perm(): return lax.ppermute(value, 'seq', pairs)]
    select_n x2 -> x0, local copies, waits for them, and re-layouts: 24.8 us -> none  [shards(): matrix = jnp.where(inside[None], banded, jnp.zeros_like(banded))]
    pallas_call x0 -> x6, Pallas kernels: none -> 18.9 us  [the longest x1 10.5 us: attend(): pl.pallas_call(kernel, out_shape=[jax.ShapeDtypeStruct((rows, part), jnp....]
    ppermute x7 -> x15, starting transfers between devices: 19.6 us -> 25.1 us  [the longest x12 17.8 us: ring_perm(): return lax.ppermute(value, 'seq', pairs)]
    ppermute x3 -> x0, local copies, waits for them, and re-layouts: 5.21 us -> none  [from_behind(): lax.ppermute(value, axis, [(source, source + steps) for source in range(i...]
    reduce_sum x2 -> x0, other arithmetic: 4.44 us -> none  [accumulate(): total = total * factor + jnp.sum(weight, axis=2)]
    reshape x2 -> x0, local copies, waits for them, and re-layouts: 2.65 us -> none  [shards(): filt.reshape(taps_count, width)]
  transfers between devices with their start and end apart: 7 -> 15, of which waited for: 5 -> 8; matrix products, arithmetic and copies ran while one was open for 46% -> 1% of each run, Pallas kernels for 0% -> 7%
where the time goes in v1:
time: 107 us
  waiting for transfers between devices  49.6 us (46%)
  starting transfers between devices  25.1 us (23%)
  Pallas kernels  18.9 us (18%)
  local copies, waits for them, and re-layouts  5.6 us (5%)
  other arithmetic  3.77 us (4%)
  blocking collectives  2.47 us (2%)
    ppermute x12, waiting for transfers between devices, ring_perm(): return lax.ppermute(value, 'seq', pairs)  29.5 us
    ppermute x3, waiting for transfers between devices, ahead(): lax.ppermute(value, 'seq', [(i, i + step) for i in range(count - step)])  20.1 us
    ppermute x12, starting transfers between devices, ring_perm(): return lax.ppermute(value, 'seq', pairs)  17.8 us
    pallas_call x1, Pallas kernels, attend(): pl.pallas_call(kernel, out_shape=[jax.ShapeDtypeStruct((rows, part), jnp....  10.5 us
    ppermute x3, starting transfers between devices, ahead(): lax.ppermute(value, 'seq', [(i, i + step) for i in range(count - step)])  7.23 us
    pallas_call x1, Pallas kernels, convolve(): pl.pallas_call(kernel, out_shape=[jax.ShapeDtypeStruct((rows, width), jnp...  6.02 us
    unnamed x22, local copies, waits for them, and re-layouts  5.05 us
    psum x1, blocking collectives, shards(): energy = lax.psum(jnp.sum(wide * wide, axis=1), 'ch')  2.47 us
  transfers between devices with their start and end apart: 15, of which 8 were waited for; matrix products, arithmetic and copies ran while one was open for 1% of the time, Pallas kernels for 7%

profile of v1, /device:TPU:128, one launch (start us, length us, event | category | flops | bytes accessed | tf_op | source)
XLA Modules:
  0.0 106.5 jit_solution(14514302913149069016)
XLA Ops:
  0.6 0.0 copy-start
  0.6 0.0 copy-start.1
  0.6 1.7 %multiply_reduce_fusion = f32[256]{0:T(256)S(1)} fusion(bf16[256,2048]{1,0:T(8,128)(2,1)} %x_ref.1), kind=kLoop, calls=%fused_computation | loop fusion | flops 1572608 | bytes 1049600 | tf_op jit(solution)/shard_map/reduce_sum | solution.py:326
  2.3 2.5 %psum.7 = f32[256]{0:T(256)S(1)} all-reduce(f32[256]{0:T(256)S(1)} %multiply_reduce_fusion), channel_id=1, replica_groups=mesh['seq'=128,'ch'=2] {'ch'}, use_global_device_ids=true, to_apply=%region_1.0 | all-reduce | flops 256 | bytes 2048 | tf_op jit(solution)/shard_map/psum | solution.py:326
  4.8 0.0 copy-done
  4.8 1.7 %multiply_convert_fusion = bf16[128,2048]{1,0:T(8,128)(2,1)} fusion(f32[2048]{0:T(1024)} %param.8, f32[128]{0:T(128)S(1)} %slice.7, bf16[256,2048]{1,0:T(8,128)(2,1)S(1)} %copy-done), kind=kLoop, calls=%fused_computation.1 | loop fusion | flops 1048576 | bytes 1057280 | tf_op jit(solution)/shard_map/convert_element_type | solution.py:333
  6.5 3.4 %collective-permute-start = (bf16[128,2048]{1,0:T(8,128)(2,1)}, bf16[128,2048]{1,0:T(8,128)(2,1)S(1)}, u32[]{:S(2)}, u32[]{:S(2)}) collective-permute-start(bf16[128,2048]{1,0:T(8,128)(2,1)} %multiply_convert_fusion), channel_id=1, source_target_pairs={{0,2},{2,4},{4,6},{6,8},{8,10},{10,12},{12,14},{14,16},{16,18},{18... | collective-permute-start | bytes 1572872 | tf_op jit(solution)/shard_map/ppermute | solution.py:320
  9.9 0.0 copy-done.1
  9.9 0.0 copy-start.2
  9.9 1.2 %copy-done.2 = bf16[256,2048]{1,0:T(8,128)(2,1)S(1)} copy-done((bf16[256,2048]{1,0:T(8,128)(2,1)S(1)}, bf16[256,2048]{1,0:T(8,128)(2,1)}, u32[]{:S(2)}) %copy-start.2) | copy-done | bytes 1048600
  11.1 1.2 %quarters.1 = (bf16[256,512]{1,0:T(8,128)(2,1)S(1)}, bf16[256,512]{1,0:T(8,128)(2,1)}, bf16[256,512]{1,0:T(8,128)(2,1)}, bf16[256,512]{1,0:T(8,128)(2,1)}, bf16[...) custom-call(s32[1]{0:T(128)} %bitcast.place_ref, ...), custom_call_target="tpu_custom_call" | custom-call | bytes 4194304 | tf_op jit(solution)/shard_map/quarters/pallas_call | solution.py:57
  12.3 0.0 copy-start.7
  12.4 0.7 copy-done.7
  13.0 1.5 %collective-permute-start.4 = (bf16[256,512]{1,0:T(8,128)(2,1)}, bf16[256,512]{1,0:T(8,128)(2,1)S(1)}, u32[]{:S(2)}, u32[]{:S(2)}) collective-permute-start(bf16[256,512]{1,0:T(8,128)(2,1)} %get-tuple-element.25), channel_id=1, source_target_pairs={{0,2},{2,4},{4,6},{6,0},{8,10},{10,12},{12,14},{14,8},{16,18},{18,... | collective-permute-start | bytes 786440 | tf_op jit(solution)/shard_map/ppermute | solution.py:314
  14.5 2.7 %collective-permute-start.5 = (bf16[256,512]{1,0:T(8,128)(2,1)}, bf16[256,512]{1,0:T(8,128)(2,1)S(1)}, u32[]{:S(2)}, u32[]{:S(2)}) collective-permute-start(bf16[256,512]{1,0:T(8,128)(2,1)} %get-tuple-element.26), channel_id=1, source_target_pairs={{0,4},{2,6},{4,0},{6,2},{8,12},{10,14},{12,8},{14,10},{16,20},{18,... | collective-permute-start | bytes 786440 | tf_op jit(solution)/shard_map/ppermute | solution.py:314
  17.3 1.1 %collective-permute-start.6 = (bf16[256,512]{1,0:T(8,128)(2,1)}, bf16[256,512]{1,0:T(8,128)(2,1)S(1)}, u32[]{:S(2)}, u32[]{:S(2)}) collective-permute-start(bf16[256,512]{1,0:T(8,128)(2,1)} %get-tuple-element.27), channel_id=1, source_target_pairs={{0,6},{2,0},{4,2},{6,4},{8,14},{10,8},{12,10},{14,12},{16,22},{18,... | collective-permute-start | bytes 786440 | tf_op jit(solution)/shard_map/ppermute | solution.py:314
  18.4 0.0 copy-done.10
  18.4 0.1 copy.11
  18.5 0.1 reduce-window.9
  18.6 0.1 reduce
  18.7 0.1 select_reduce_fusion.1
  18.8 0.0 copy-done.9
  18.8 0.1 rev.3
  18.9 9.2 %collective-permute-done.tail_ref = bf16[128,2048]{1,0:T(8,128)(2,1)S(1)} collective-permute-done((bf16[128,2048]{1,0:T(8,128)(2,1)}, bf16[128,2048]{1,0:T(8,128)(2,1)S(1)}, u32[]{:S(2)}, u32[]{:S(2)}) %collective-permute-start) | collective-permute-done | bytes 524320 | tf_op jit(solution)/shard_map/ppermute | solution.py:320
  28.1 0.1 broadcast_in_dim.27.begin_ref
  28.2 0.1 broadcast_in_dim.24.rms_ref
  28.3 0.0 copy-done.5
  28.3 0.0 copy-start.6
  28.3 1.2 %copy-done.6 = bf16[256,2048]{1,0:T(8,128)(2,1)S(1)} copy-done((bf16[256,2048]{1,0:T(8,128)(2,1)S(1)}, bf16[256,2048]{1,0:T(8,128)(2,1)}, u32[]{:S(2)}) %copy-start.6) | copy-done | bytes 1048600
  29.5 6.0 %convolve.1 = (bf16[256,2048]{1,0:T(8,128)(2,1)}, bf16[256,512]{1,0:T(8,128)(2,1)S(1)}, bf16[256,512]{1,0:T(8,128)(2,1)S(1)}, bf16[256,512]{1,0:T(8,128)(2,1)S(1)}, bf16[256,512]{1,0:T(8,128)(2,1)S(1)}) custom-call(s32[1]{0:T(128)} %bitcast.place_ref, bf16[256,2048]{1,0:T(8,128)(2,1)S(1)} %copy-done, bf16[128,2048]{1,0:T(8,128)(2,1)S(1)} %collective-permute-done.tail_ref, ...), custom_call_target="tpu_custom_call" | custom-call | flops 2147483648 | bytes 5242880 | tf_op jit(solution)/shard_map/convolve/pallas_call | solution.py:188
  35.6 0.0 collective-permute-start.7
  35.6 0.0 collective-permute-start.8
  35.6 0.0 collective-permute-done.4.refs_1_.refs_5_
  35.6 3.2 %collective-permute-start.9 = (bf16[256,512]{1,0:T(8,128)(2,1)S(1)}, bf16[256,512]{1,0:T(8,128)(2,1)S(1)}, u32[]{:S(2)}, u32[]{:S(2)}) collective-permute-start(bf16[256,512]{1,0:T(8,128)(2,1)S(1)} %get-tuple-element.31), channel_id=1, source_target_pairs={{0,6},{2,0},{4,2},{6,4},{8,14},{10,8},{12,10},{14,12},{16,22},{18,... | collective-permute-start | bytes 786440 | tf_op jit(solution)/shard_map/ppermute | solution.py:314
  38.8 0.0 collective-permute-done.5.refs_2_.refs_6_
  38.8 0.0 collective-permute-done.6.refs_3_.refs_7_
  38.8 0.1 last_shards.2
  38.9 1.9 %collective-permute-start.10 = (bf16[768,512]{1,0:T(8,128)(2,1)S(1)}, bf16[768,512]{1,0:T(8,128)(2,1)}, u32[]{:S(2)}, u32[]{:S(2)}) collective-permute-start(bf16[768,512]{1,0:T(8,128)(2,1)S(1)} %last_shards.2), channel_id=1, source_target_pairs={{0,8},{2,10},{4,12},{6,14},{8,16},{10,18},{12,20},{14,22},{16,24},... | collective-permute-start | bytes 2359304 | tf_op jit(solution)/shard_map/ppermute | solution.py:320
  40.9 9.0 %collective-permute-done.7.refs_1_.refs_9_ = bf16[256,512]{1,0:T(8,128)(2,1)S(1)} collective-permute-done((bf16[256,512]{1,0:T(8,128)(2,1)S(1)}, bf16[256,512]{1,0:T(8,128)(2,1)S(1)}, u32[]{:S(2)}, u32[]{:S(2)}) %collective-permute-start.7) | collective-permute-done | bytes 262176 | tf_op jit(solution)/shard_map/ppermute | solution.py:314
  49.9 0.0 collective-permute-done.8.refs_2_.refs_10_
  49.9 0.6 collective-permute-done.9.refs_3_.refs_11_
  50.5 0.1 last_shards.3
  50.6 1.9 %collective-permute-start.11 = (bf16[768,512]{1,0:T(8,128)(2,1)S(1)}, bf16[768,512]{1,0:T(8,128)(2,1)}, u32[]{:S(2)}, u32[]{:S(2)}) collective-permute-start(bf16[768,512]{1,0:T(8,128)(2,1)S(1)} %last_shards.3), channel_id=1, source_target_pairs={{0,8},{2,10},{4,12},{6,14},{8,16},{10,18},{12,20},{14,22},{16,24},... | collective-permute-start | bytes 2359304 | tf_op jit(solution)/shard_map/ppermute | solution.py:320
  52.5 0.3 collective-permute-start.1
  52.9 3.6 %collective-permute-start.2 = (bf16[256,512]{1,0:T(8,128)(2,1)}, bf16[256,512]{1,0:T(8,128)(2,1)}, u32[]{:S(2)}, u32[]{:S(2)}) collective-permute-start(bf16[256,512]{1,0:T(8,128)(2,1)} %get-tuple-element.22), channel_id=1, source_target_pairs={{0,4},{2,6},{4,0},{6,2},{8,12},{10,14},{12,8},{14,10},{16,20},{18,... | collective-permute-start | bytes 786440 | tf_op jit(solution)/shard_map/ppermute | solution.py:314
  56.4 0.0 collective-permute-start.3
  56.4 0.1 select_reduce_fusion
  56.6 5.0 %collective-permute-done.1.refs_1_ = bf16[256,512]{1,0:T(8,128)(2,1)} collective-permute-done((bf16[256,512]{1,0:T(8,128)(2,1)}, bf16[256,512]{1,0:T(8,128)(2,1)}, u32[]{:S(2)}, u32[]{:S(2)}) %collective-permute-start.1) | collective-permute-done | bytes 262176 | tf_op jit(solution)/shard_map/ppermute | solution.py:314
  61.6 6.7 %collective-permute-done.2.refs_2_ = bf16[256,512]{1,0:T(8,128)(2,1)} collective-permute-done((bf16[256,512]{1,0:T(8,128)(2,1)}, bf16[256,512]{1,0:T(8,128)(2,1)}, u32[]{:S(2)}, u32[]{:S(2)}) %collective-permute-start.2) | collective-permute-done | bytes 262176 | tf_op jit(solution)/shard_map/ppermute | solution.py:314
  68.3 0.0 collective-permute-done.3.refs_3_
  68.3 0.0 collective-permute-done.10.refs_12_
  68.3 10.9 %collective-permute-done.11.refs_13_ = bf16[768,512]{1,0:T(8,128)(2,1)} collective-permute-done((bf16[768,512]{1,0:T(8,128)(2,1)S(1)}, bf16[768,512]{1,0:T(8,128)(2,1)}, u32[]{:S(2)}, u32[]{:S(2)}) %collective-permute-start.11) | collective-permute-done | bytes 786464 | tf_op jit(solution)/shard_map/ppermute | solution.py:320
  79.3 0.2 broadcast_in_dim.33.begin_ref
  79.5 0.0 copy-start.4
  79.5 0.9 copy-done.4
  80.4 0.9 copy-done.8
  81.4 10.5 %attend.1 = (bf16[256,512]{1,0:T(8,128)(2,1)S(1)}, bf16[256,512]{1,0:T(8,128)(2,1)S(1)}, bf16[256,512]{1,0:T(8,128)(2,1)S(1)}, bf16[256,512]{1,0:T(8,128)(2,1)S(1)}) custom-call(s32[1]{0:T(128)} %bitcast.place_ref, s32[1024,128]{1,0:T(8,128)S(1)} %broadcast_in_dim.33.begin_ref, bf16[256,512]{1,0:T(8,128)(2,1)S(1)} %copy-done.8, ...), custom_call_target="tpu_custom_call" | custom-call | flops 8589934592 | bytes 8388608 | tf_op jit(solution)/shard_map/attend/pallas_call | solution.py:279
  91.9 1.0 collective-permute-start.12
  92.8 1.9 %collective-permute-start.13 = (bf16[256,512]{1,0:T(8,128)(2,1)S(1)}, bf16[256,512]{1,0:T(8,128)(2,1)S(1)}, u32[]{:S(2)}, u32[]{:S(2)}) collective-permute-start(bf16[256,512]{1,0:T(8,128)(2,1)S(1)} %get-tuple-element.34), channel_id=1, source_target_pairs={{0,4},{2,6},{4,0},{6,2},{8,12},{10,14},{12,8},{14,10},{16,20},{18,... | collective-permute-start | bytes 786440 | tf_op jit(solution)/shard_map/ppermute | solution.py:314
  94.7 2.5 %collective-permute-start.14 = (bf16[256,512]{1,0:T(8,128)(2,1)S(1)}, bf16[256,512]{1,0:T(8,128)(2,1)S(1)}, u32[]{:S(2)}, u32[]{:S(2)}) collective-permute-start(bf16[256,512]{1,0:T(8,128)(2,1)S(1)} %get-tuple-element.35), channel_id=1, source_target_pairs={{0,6},{2,0},{4,2},{6,4},{8,14},{10,8},{12,10},{14,12},{16,22},{18,... | collective-permute-start | bytes 786440 | tf_op jit(solution)/shard_map/ppermute | solution.py:314
  97.2 7.5 %collective-permute-done.12.refs_1_ = bf16[256,512]{1,0:T(8,128)(2,1)S(1)} collective-permute-done((bf16[256,512]{1,0:T(8,128)(2,1)S(1)}, bf16[256,512]{1,0:T(8,128)(2,1)S(1)}, u32[]{:S(2)}, u32[]{:S(2)}) %collective-permute-start.12) | collective-permute-done | bytes 262176 | tf_op jit(solution)/shard_map/ppermute | solution.py:314
  104.8 0.0 collective-permute-done.13.refs_2_
  104.8 0.6 collective-permute-done.14.refs_3_
  105.4 1.0 whole_width.1
  (14 shorter events, 0.1 us)
Async XLA Ops:
  0.6 4.2 %copy-start = (bf16[256,2048]{1,0:T(8,128)(2,1)S(1)}, bf16[256,2048]{1,0:T(8,128)(2,1)}, u32[]{:S(2)}) copy-start(bf16[256,2048]{1,0:T(8,128)(2,1)} %x_ref.1) | copy-start | bytes 3145732
  0.6 9.2 %copy-start.1 = (bf16[256,2048]{1,0:T(8,128)(2,1)S(1)}, bf16[256,2048]{1,0:T(8,128)(2,1)}, u32[]{:S(2)}) copy-start(bf16[256,2048]{1,0:T(8,128)(2,1)} %refs_0_.1) | copy-start | bytes 3145732
  6.5 21.6 %collective-permute-start = (bf16[128,2048]{1,0:T(8,128)(2,1)}, bf16[128,2048]{1,0:T(8,128)(2,1)S(1)}, u32[]{:S(2)}, u32[]{:S(2)}) collective-permute-start(bf16[128,2048]{1,0:T(8,128)(2,1)} %multiply_convert_fusion), channel_id=1, source_target_pairs={{0,2},{2,4},{4,6},{6,8},{8,10},{10,12},{12,14},{14,16},{16,18},{18... | collective-permute-start | bytes 1572872 | tf_op jit(solution)/shard_map/ppermute | solution.py:320
  9.9 1.2 %copy-start.2 = (bf16[256,2048]{1,0:T(8,128)(2,1)S(1)}, bf16[256,2048]{1,0:T(8,128)(2,1)}, u32[]{:S(2)}) copy-start(bf16[256,2048]{1,0:T(8,128)(2,1)} %refs_1_.1) | copy-start | bytes 3145732
  11.1 7.3 %copy-start.10 = (s32[48]{0:T(128)S(1)}, s32[48]{0:T(128)}, u32[]{:S(2)}) copy-start(s32[48]{0:T(128)} %param.13) | copy-start | bytes 580
  11.1 7.7 %copy-start.9 = (bf16[128,128]{1,0:T(8,128)(2,1)S(1)}, bf16[128,128]{1,0:T(8,128)(2,1)}, u32[]{:S(2)}) copy-start(bf16[128,128]{1,0:T(8,128)(2,1)} %param.9) | copy-start | bytes 98308
  11.1 17.2 %copy-start.5 = (f32[2048]{0:T(1024)S(1)}, f32[2048]{0:T(1024)}, u32[]{:S(2)}) copy-start(f32[2048]{0:T(1024)} %param.8) | copy-start | bytes 24580
  12.3 0.7 copy-start.7
  13.0 22.5 %collective-permute-start.4 = (bf16[256,512]{1,0:T(8,128)(2,1)}, bf16[256,512]{1,0:T(8,128)(2,1)S(1)}, u32[]{:S(2)}, u32[]{:S(2)}) collective-permute-start(bf16[256,512]{1,0:T(8,128)(2,1)} %get-tuple-element.25), channel_id=1, source_target_pairs={{0,2},{2,4},{4,6},{6,0},{8,10},{10,12},{12,14},{14,8},{16,18},{18,... | collective-permute-start | bytes 786440 | tf_op jit(solution)/shard_map/ppermute | solution.py:314
  14.5 24.3 %collective-permute-start.5 = (bf16[256,512]{1,0:T(8,128)(2,1)}, bf16[256,512]{1,0:T(8,128)(2,1)S(1)}, u32[]{:S(2)}, u32[]{:S(2)}) collective-permute-start(bf16[256,512]{1,0:T(8,128)(2,1)} %get-tuple-element.26), channel_id=1, source_target_pairs={{0,4},{2,6},{4,0},{6,2},{8,12},{10,14},{12,8},{14,10},{16,20},{18,... | collective-permute-start | bytes 786440 | tf_op jit(solution)/shard_map/ppermute | solution.py:314
  17.3 21.5 %collective-permute-start.6 = (bf16[256,512]{1,0:T(8,128)(2,1)}, bf16[256,512]{1,0:T(8,128)(2,1)S(1)}, u32[]{:S(2)}, u32[]{:S(2)}) collective-permute-start(bf16[256,512]{1,0:T(8,128)(2,1)} %get-tuple-element.27), channel_id=1, source_target_pairs={{0,6},{2,0},{4,2},{6,4},{8,14},{10,8},{12,10},{14,12},{16,22},{18,... | collective-permute-start | bytes 786440 | tf_op jit(solution)/shard_map/ppermute | solution.py:314
  28.3 1.2 %copy-start.6 = (bf16[256,2048]{1,0:T(8,128)(2,1)S(1)}, bf16[256,2048]{1,0:T(8,128)(2,1)}, u32[]{:S(2)}) copy-start(bf16[256,2048]{1,0:T(8,128)(2,1)} %gate_ref.1) | copy-start | bytes 3145732
  35.6 14.3 %collective-permute-start.7 = (bf16[256,512]{1,0:T(8,128)(2,1)S(1)}, bf16[256,512]{1,0:T(8,128)(2,1)S(1)}, u32[]{:S(2)}, u32[]{:S(2)}) collective-permute-start(bf16[256,512]{1,0:T(8,128)(2,1)S(1)} %get-tuple-element.29), channel_id=1, source_target_pairs={{0,2},{2,4},{4,6},{6,0},{8,10},{10,12},{12,14},{14,8},{16,18},{18,... | collective-permute-start | bytes 786440 | tf_op jit(solution)/shard_map/ppermute | solution.py:314
  35.6 14.3 %collective-permute-start.8 = (bf16[256,512]{1,0:T(8,128)(2,1)S(1)}, bf16[256,512]{1,0:T(8,128)(2,1)S(1)}, u32[]{:S(2)}, u32[]{:S(2)}) collective-permute-start(bf16[256,512]{1,0:T(8,128)(2,1)S(1)} %get-tuple-element.30), channel_id=1, source_target_pairs={{0,4},{2,6},{4,0},{6,2},{8,12},{10,14},{12,8},{14,10},{16,20},{18,... | collective-permute-start | bytes 786440 | tf_op jit(solution)/shard_map/ppermute | solution.py:314
  35.6 14.9 %collective-permute-start.9 = (bf16[256,512]{1,0:T(8,128)(2,1)S(1)}, bf16[256,512]{1,0:T(8,128)(2,1)S(1)}, u32[]{:S(2)}, u32[]{:S(2)}) collective-permute-start(bf16[256,512]{1,0:T(8,128)(2,1)S(1)} %get-tuple-element.31), channel_id=1, source_target_pairs={{0,6},{2,0},{4,2},{6,4},{8,14},{10,8},{12,10},{14,12},{16,22},{18,... | collective-permute-start | bytes 786440 | tf_op jit(solution)/shard_map/ppermute | solution.py:314
  38.9 29.4 %collective-permute-start.10 = (bf16[768,512]{1,0:T(8,128)(2,1)S(1)}, bf16[768,512]{1,0:T(8,128)(2,1)}, u32[]{:S(2)}, u32[]{:S(2)}) collective-permute-start(bf16[768,512]{1,0:T(8,128)(2,1)S(1)} %last_shards.2), channel_id=1, source_target_pairs={{0,8},{2,10},{4,12},{6,14},{8,16},{10,18},{12,20},{14,22},{16,24},... | collective-permute-start | bytes 2359304 | tf_op jit(solution)/shard_map/ppermute | solution.py:320
  50.5 2.1 %copy-start.3 = (bf16[256,512]{1,0:T(8,128)(2,1)}, bf16[256,512]{1,0:T(8,128)(2,1)S(1)}, u32[]{:S(2)}) copy-start(bf16[256,512]{1,0:T(8,128)(2,1)S(1)} %collective-permute-done.9.refs_3_.refs_11_) | copy-start | bytes 786436
  50.6 28.6 %collective-permute-start.11 = (bf16[768,512]{1,0:T(8,128)(2,1)S(1)}, bf16[768,512]{1,0:T(8,128)(2,1)}, u32[]{:S(2)}, u32[]{:S(2)}) collective-permute-start(bf16[768,512]{1,0:T(8,128)(2,1)S(1)} %last_shards.3), channel_id=1, source_target_pairs={{0,8},{2,10},{4,12},{6,14},{8,16},{10,18},{12,20},{14,22},{16,24},... | collective-permute-start | bytes 2359304 | tf_op jit(solution)/shard_map/ppermute | solution.py:320
  52.5 9.0 %collective-permute-start.1 = (bf16[256,512]{1,0:T(8,128)(2,1)}, bf16[256,512]{1,0:T(8,128)(2,1)}, u32[]{:S(2)}, u32[]{:S(2)}) collective-permute-start(bf16[256,512]{1,0:T(8,128)(2,1)} %get-tuple-element.21), channel_id=1, source_target_pairs={{0,2},{2,4},{4,6},{6,0},{8,10},{10,12},{12,14},{14,8},{16,18},{18,... | collective-permute-start | bytes 786440 | tf_op jit(solution)/shard_map/ppermute | solution.py:314
  52.9 15.4 %collective-permute-start.2 = (bf16[256,512]{1,0:T(8,128)(2,1)}, bf16[256,512]{1,0:T(8,128)(2,1)}, u32[]{:S(2)}, u32[]{:S(2)}) collective-permute-start(bf16[256,512]{1,0:T(8,128)(2,1)} %get-tuple-element.22), channel_id=1, source_target_pairs={{0,4},{2,6},{4,0},{6,2},{8,12},{10,14},{12,8},{14,10},{16,20},{18,... | collective-permute-start | bytes 786440 | tf_op jit(solution)/shard_map/ppermute | solution.py:314
  56.4 11.9 %collective-permute-start.3 = (bf16[256,512]{1,0:T(8,128)(2,1)}, bf16[256,512]{1,0:T(8,128)(2,1)}, u32[]{:S(2)}, u32[]{:S(2)}) collective-permute-start(bf16[256,512]{1,0:T(8,128)(2,1)} %get-tuple-element.23), channel_id=1, source_target_pairs={{0,6},{2,0},{4,2},{6,4},{8,14},{10,8},{12,10},{14,12},{16,22},{18,... | collective-permute-start | bytes 786440 | tf_op jit(solution)/shard_map/ppermute | solution.py:314
  79.5 1.0 copy-start.4
  80.4 0.9 copy-start.8
  91.9 12.9 %collective-permute-start.12 = (bf16[256,512]{1,0:T(8,128)(2,1)S(1)}, bf16[256,512]{1,0:T(8,128)(2,1)S(1)}, u32[]{:S(2)}, u32[]{:S(2)}) collective-permute-start(bf16[256,512]{1,0:T(8,128)(2,1)S(1)} %get-tuple-element.33), channel_id=1, source_target_pairs={{0,2},{2,4},{4,6},{6,0},{8,10},{10,12},{12,14},{14,8},{16,18},{18,... | collective-permute-start | bytes 786440 | tf_op jit(solution)/shard_map/ppermute | solution.py:314
  92.8 11.9 %collective-permute-start.13 = (bf16[256,512]{1,0:T(8,128)(2,1)S(1)}, bf16[256,512]{1,0:T(8,128)(2,1)S(1)}, u32[]{:S(2)}, u32[]{:S(2)}) collective-permute-start(bf16[256,512]{1,0:T(8,128)(2,1)S(1)} %get-tuple-element.34), channel_id=1, source_target_pairs={{0,4},{2,6},{4,0},{6,2},{8,12},{10,14},{12,8},{14,10},{16,20},{18,... | collective-permute-start | bytes 786440 | tf_op jit(solution)/shard_map/ppermute | solution.py:314
  94.7 10.7 %collective-permute-start.14 = (bf16[256,512]{1,0:T(8,128)(2,1)S(1)}, bf16[256,512]{1,0:T(8,128)(2,1)S(1)}, u32[]{:S(2)}, u32[]{:S(2)}) collective-permute-start(bf16[256,512]{1,0:T(8,128)(2,1)S(1)} %get-tuple-element.35), channel_id=1, source_target_pairs={{0,6},{2,0},{4,2},{6,4},{8,14},{10,8},{12,10},{14,12},{16,22},{18,... | collective-permute-start | bytes 786440 | tf_op jit(solution)/shard_map/ppermute | solution.py:314

commit v2 on v1

v2 whole, which is shorter than its diff:
```python
import jax
import jax.numpy as jnp
from jax import lax
from jax.experimental import pallas as pl
from jax.experimental.pallas import tpu as pltpu
from jax.sharding import PartitionSpec as P

HEAD_DIM = 128
GROUP = 16
TAPS = 128
CONV_CH = 4096
RING = 4
CUTS = 1
MIB = 1024 * 1024
HBM = pl.BlockSpec(memory_space=pltpu.HBM)
SMEM = pl.BlockSpec(memory_space=pltpu.SMEM)
VMEM = pl.BlockSpec(memory_space=pltpu.VMEM)
NEG = -1e30


def begin_of(doc_lengths, positions):
    ends = jnp.cumsum(doc_lengths)
    starts = ends - doc_lengths
    inside = starts[None, :] <= positions[:, None]
    return jnp.max(jnp.where(inside, starts[None, :], 0), axis=1)


def params(mib):
    return pltpu.CompilerParams(vmem_limit_bytes=mib * MIB)


def quarters(place, *arrays):
    rows, width = arrays[0].shape
    part = width // RING
    count = len(arrays)

    def kernel(place_ref, *refs):
        ins, outs, sem = refs[:count], refs[count : count + count * RING], refs[-1]
        place = place_ref[0]
        copies = []
        for a in range(count):
            for d in range(RING):
                low = pl.multiple_of(lax.rem(place + d, RING) * part, part)
                copies.append(
                    pltpu.make_async_copy(
                        ins[a].at[:, pl.ds(low, part)], outs[a * RING + d], sem.at[a * RING + d]
                    )
                )
        for copy in copies:
            copy.start()
        for copy in copies:
            copy.wait()

    out = pl.pallas_call(
        kernel,
        out_shape=[
            jax.ShapeDtypeStruct((rows, part), arrays[0].dtype) for _ in range(count * RING)
        ],
        in_specs=[SMEM] + [HBM] * count,
        out_specs=[VMEM] * (count * RING),
        scratch_shapes=[pltpu.SemaphoreType.DMA((count * RING,))],
        compiler_params=params(8),
        name="quarters",
    )(place, *arrays)
    return [out[a * RING : (a + 1) * RING] for a in range(count)]


def whole_width(place, sets):
    rows, width = sets[0][0].shape
    cuts = len(sets)

    def kernel(place_ref, *refs):
        ins, out, sem = refs[: RING * cuts], refs[RING * cuts], refs[-1]
        place = place_ref[0]
        copies = []
        for c in range(cuts):
            for d in range(RING):
                at = c * RING + d
                low = (lax.rem(place + RING - d, RING) * cuts + c) * width
                cols = pl.ds(pl.multiple_of(low, width), width)
                copies.append(pltpu.make_async_copy(ins[at], out.at[:, cols], sem.at[at]))
        for copy in copies:
            copy.start()
        for copy in copies:
            copy.wait()

    return pl.pallas_call(
        kernel,
        out_shape=jax.ShapeDtypeStruct((rows, width * cuts * RING), sets[0][0].dtype),
        in_specs=[SMEM] + [VMEM] * (RING * cuts),
        out_specs=HBM,
        scratch_shapes=[pltpu.SemaphoreType.DMA((RING * cuts,))],
        compiler_params=params(8),
        name="whole_width",
    )(place, *[piece for pieces in sets for piece in pieces])


def last_shards(place, pieces, cuts):
    rows, part = pieces[0].shape
    width = part // cuts

    def kernel(place_ref, *refs):
        ins, outs, sem = refs[:RING], refs[RING : RING + cuts], refs[-1]
        place = place_ref[0]

        def copy_of(d, c):
            shard = lax.rem(place + RING - d, RING)
            low = pl.multiple_of(jnp.maximum(shard - 1, 0) * rows, rows)
            return shard, pltpu.make_async_copy(
                ins[d].at[:, pl.ds(c * width, width)],
                outs[c].at[pl.ds(low, rows), :],
                sem.at[d * cuts + c],
            )

        every = [(d, c) for d in range(RING) for c in range(cuts)]
        for d, c in every:
            shard, copy = copy_of(d, c)
            pl.when(shard > 0)(copy.start)
        for d, c in every:
            shard, copy = copy_of(d, c)
            pl.when(shard > 0)(copy.wait)

    return pl.pallas_call(
        kernel,
        out_shape=[
            jax.ShapeDtypeStruct((rows * (RING - 1), width), pieces[0].dtype) for _ in range(cuts)
        ],
        in_specs=[SMEM] + [VMEM] * RING,
        out_specs=[VMEM] * cuts,
        scratch_shapes=[pltpu.SemaphoreType.DMA((RING * cuts,))],
        compiler_params=params(8),
        name="last_shards",
    )(place, *pieces)


def convolve_own(place, conv_in, rms, gain, taps, gate, begin):
    rows, width = conv_in.shape
    lanes = 128
    per = lanes // GROUP
    blocks = rows // TAPS

    def kernel(x_ref, rms_ref, gain_ref, taps_ref, gate_ref, begin_ref, *refs):
        mixed_ref, part_ref, band_ref, masks, src, lhs = refs
        out_row = lax.broadcasted_iota(jnp.int32, (TAPS, lanes), 0)
        src_col = lax.broadcasted_iota(jnp.int32, (TAPS, lanes), 1)
        for b in range(blocks):
            first = begin_ref[b * TAPS : (b + 1) * TAPS, :]
            low = b * TAPS
            before = (src_col > out_row) & (src_col + (low - TAPS) >= first)
            inside = (src_col <= out_row) & (src_col + low >= first)
            masks[2 * b] = jnp.where(before, 1.0, 0.0).astype(jnp.bfloat16)
            masks[2 * b + 1] = jnp.where(inside, 1.0, 0.0).astype(jnp.bfloat16)
        lane_group = lax.broadcasted_iota(jnp.int32, (TAPS, lanes), 1) // GROUP

        def pick(full):
            picked = full[:TAPS]
            for j in range(1, per):
                picked = jnp.where(lane_group == j, full[j * TAPS : (j + 1) * TAPS], picked)
            return picked

        for at in range(width // lanes):
            cols = slice(at * lanes, (at + 1) * lanes)
            src[...] = (
                x_ref[:, cols].astype(jnp.float32) * rms_ref[...] * gain_ref[:, cols]
            ).astype(jnp.bfloat16)
            for j in range(per):
                line = jnp.broadcast_to(
                    taps_ref[at * per + j : at * per + j + 1, :], (TAPS, lanes)
                )
                band = pltpu.roll(line, 1, 1, stride=1, stride_axis=0).astype(jnp.bfloat16)
                spot = slice(j * TAPS, (j + 1) * TAPS)
                band_ref[at, spot, :] = band * masks[0]
                lhs[0, spot, :lanes] = band * masks[1]
                for b in range(1, blocks):
                    lhs[b, spot, :lanes] = band * masks[2 * b]
                    lhs[b, spot, lanes:] = band * masks[2 * b + 1]
            part_ref[:, cols] = pick(
                jnp.dot(lhs[0, :, :lanes], src[:TAPS, :], preferred_element_type=jnp.float32)
            )
            for b in range(1, blocks):
                full = jnp.dot(
                    lhs[b],
                    src[(b - 1) * TAPS : (b + 1) * TAPS, :],
                    preferred_element_type=jnp.float32,
                )
                here = slice(b * TAPS, (b + 1) * TAPS)
                mixed_ref[(b - 1) * TAPS : b * TAPS, cols] = (
                    gate_ref[here, cols].astype(jnp.float32) * pick(full)
                ).astype(jnp.bfloat16)

    return pl.pallas_call(
        kernel,
        out_shape=[
            jax.ShapeDtypeStruct((rows - TAPS, width), jnp.bfloat16),
            jax.ShapeDtypeStruct((TAPS, width), jnp.float32),
            jax.ShapeDtypeStruct((width // lanes, per * TAPS, lanes), jnp.bfloat16),
        ],
        in_specs=[VMEM] * 6,
        out_specs=[VMEM] * 3,
        scratch_shapes=[
            pltpu.VMEM((2 * blocks, TAPS, lanes), jnp.bfloat16),
            pltpu.VMEM((rows, lanes), jnp.bfloat16),
            pltpu.VMEM((blocks, per * TAPS, 2 * lanes), jnp.bfloat16),
        ],
        compiler_params=params(20),
        name="convolve_own",
    )(conv_in, rms, gain, taps, gate, begin)


def convolve_tail(place, tail, part, bands, rest, gate):
    width = tail.shape[1]
    rows = TAPS + rest.shape[0]
    block = width // RING
    lanes = 128
    per = lanes // GROUP

    def kernel(place_ref, tail_ref, part_ref, band_ref, rest_ref, gate_ref, *refs):
        mixed_ref, outs = refs[0], refs[1:]
        place = place_ref[0]
        lane_group = lax.broadcasted_iota(jnp.int32, (TAPS, lanes), 1) // GROUP
        for d in range(RING):
            for c in range(block // lanes):
                at = lax.rem(place + d, RING) * (block // lanes) + c
                cols = pl.ds(pl.multiple_of(at * lanes, lanes), lanes)
                mine = slice(c * lanes, (c + 1) * lanes)
                full = jnp.dot(band_ref[at], tail_ref[:, cols], preferred_element_type=jnp.float32)
                picked = full[:TAPS]
                for j in range(1, per):
                    picked = jnp.where(lane_group == j, full[j * TAPS : (j + 1) * TAPS], picked)
                out = (
                    gate_ref[:TAPS, cols].astype(jnp.float32) * (part_ref[:, cols] + picked)
                ).astype(jnp.bfloat16)
                mixed_ref[:TAPS, cols] = out
                outs[d][:TAPS, mine] = out
                other = rest_ref[:, cols]
                mixed_ref[TAPS:, cols] = other
                outs[d][TAPS:, mine] = other

    out = pl.pallas_call(
        kernel,
        out_shape=[jax.ShapeDtypeStruct((rows, width), jnp.bfloat16)]
        + [jax.ShapeDtypeStruct((rows, block), jnp.bfloat16) for _ in range(RING)],
        in_specs=[SMEM] + [VMEM] * 5,
        out_specs=[VMEM] * (1 + RING),
        compiler_params=params(16),
        name="convolve_tail",
    )(place, tail, part, bands, rest, gate)
    return out[0], list(out[1:])


SCALE = HEAD_DIM**-0.5 * 1.4426950408889634
BOTH_LAST = (((1,), (1,)), ((), ()))


def attend_ring(place, begin, queries, keys, values):
    rows, part = queries[0].shape
    heads = part // HEAD_DIM
    span = RING * rows

    def kernel(place_ref, begin_ref, *refs):
        ins = (refs[:RING], refs[RING : 2 * RING], refs[2 * RING : 3 * RING])
        acc_ref, top_ref, total_ref, q_all, k_all, v_all, sem = refs[3 * RING :]
        alls = (q_all, k_all, v_all)
        place = place_ref[0]
        for d in range(RING):
            shard = lax.rem(place + RING - d, RING)
            low = pl.multiple_of(shard * rows, rows)
            for a in range(3):
                pltpu.make_async_copy(
                    ins[a][d], alls[a].at[pl.ds(low, rows), :], sem.at[a, shard]
                ).start()
        for s in range(RING):
            here = slice(s * rows, (s + 1) * rows)
            size = (s + 1) * rows
            for a in range(3):
                pltpu.make_async_copy(ins[a][0], alls[a].at[here, :], sem.at[a, s]).wait()
            first = begin_ref[here, :]
            key = lax.broadcasted_iota(jnp.int32, (rows, 128), 1)
            row = lax.broadcasted_iota(jnp.int32, (rows, 128), 0) + s * rows
            bias = []
            for c in range(size // 128):
                valid = key + c * 128 >= first
                if (c + 1) * 128 > s * rows:
                    valid = valid & (key + c * 128 <= row)
                bias.append(jnp.where(valid, 0.0, NEG))
            bias = jnp.concatenate(bias, axis=1)
            for h in range(heads):
                cols = slice(h * HEAD_DIM, (h + 1) * HEAD_DIM)
                score = bias + lax.dot_general(
                    q_all[here, cols],
                    k_all[:size, cols],
                    BOTH_LAST,
                    preferred_element_type=jnp.float32,
                )
                top = jnp.max(score, axis=1, keepdims=True)
                weight = jnp.exp2((score - top) * SCALE)
                total = jnp.sum(weight, axis=1, keepdims=True)
                acc_ref[here, cols] = jnp.dot(
                    weight.astype(jnp.bfloat16),
                    v_all[:size, cols],
                    preferred_element_type=jnp.float32,
                )
                top_ref[here, cols] = jnp.broadcast_to(top, (rows, HEAD_DIM))
                total_ref[here, cols] = jnp.broadcast_to(total, (rows, HEAD_DIM))

    return pl.pallas_call(
        kernel,
        out_shape=[jax.ShapeDtypeStruct((span, part), jnp.float32) for _ in range(3)]
        + [jax.ShapeDtypeStruct((span, part), jnp.bfloat16)],
        in_specs=[SMEM] + [VMEM] * (1 + 3 * RING),
        out_specs=[VMEM] * 4,
        scratch_shapes=[
            pltpu.VMEM((span, part), jnp.bfloat16),
            pltpu.VMEM((span, part), jnp.bfloat16),
            pltpu.SemaphoreType.DMA((3, RING)),
        ],
        compiler_params=params(20),
        name="attend_ring",
    )(place, begin, *queries, *keys, *values)


def attend_halo(place, begin, sums, queries, key_halo, value_halo):
    back, part = value_halo.shape
    rows = back // (RING - 1)
    heads = part // HEAD_DIM
    span = RING * rows

    def kernel(place_ref, begin_ref, acc_ref, top_ref, total_ref, q_ref, k_ref, v_ref, *refs):
        outs, o_all, sem = refs[:RING], refs[RING], refs[RING + 1]
        place = place_ref[0]
        for s in (3, 0, 1, 2):
            here = slice(s * rows, (s + 1) * rows)
            size = (RING - 1 - s) * rows
            low = s * rows
            if size:
                first = begin_ref[here, :]
                key = lax.broadcasted_iota(jnp.int32, (rows, 128), 1) + (low - back)
                bias = jnp.concatenate(
                    [jnp.where(key + c * 128 >= first, 0.0, NEG) for c in range(size // 128)],
                    axis=1,
                )
            for h in range(heads):
                cols = slice(h * HEAD_DIM, (h + 1) * HEAD_DIM)
                top = top_ref[here, cols]
                total = total_ref[here, cols]
                out = acc_ref[here, cols]
                if size:
                    score = bias + lax.dot_general(
                        q_ref[here, cols],
                        k_ref[low:, cols],
                        BOTH_LAST,
                        preferred_element_type=jnp.float32,
                    )
                    new_top = jnp.maximum(top, jnp.max(score, axis=1, keepdims=True))
                    wide_top = jnp.concatenate([new_top] * (size // HEAD_DIM), axis=1)
                    weight = jnp.exp2((score - wide_top) * SCALE)
                    factor = jnp.exp2((top - new_top) * SCALE)
                    total = total * factor + jnp.sum(weight, axis=1, keepdims=True)
                    out = out * factor + jnp.dot(
                        weight.astype(jnp.bfloat16),
                        v_ref[low:, cols],
                        preferred_element_type=jnp.float32,
                    )
                o_all[here, cols] = (out * (1.0 / total)).astype(jnp.bfloat16)
            for d in range(RING):
                copy = pltpu.make_async_copy(o_all.at[here, :], outs[d], sem.at[d])
                pl.when(lax.rem(place + d, RING) == s)(copy.start)
        for d in range(RING):
            pltpu.make_async_copy(o_all.at[:rows, :], outs[d], sem.at[d]).wait()

    return pl.pallas_call(
        kernel,
        out_shape=[jax.ShapeDtypeStruct((rows, part), jnp.bfloat16) for _ in range(RING)],
        in_specs=[SMEM] + [VMEM] * 7,
        out_specs=[VMEM] * RING,
        scratch_shapes=[
            pltpu.VMEM((span, part), jnp.bfloat16),
            pltpu.SemaphoreType.DMA((RING,)),
        ],
        compiler_params=params(20),
        name="attend_halo",
    )(place, begin, *sums, queries, key_halo, value_halo)


def shards(conv_in, norm_gain, filters, gate, queries, keys, doc_lengths):
    rows, width = conv_in.shape
    count = lax.axis_size("seq")
    index = lax.axis_index("seq")
    base = index * rows
    place = lax.rem(index, RING)
    ring_base = (index - place) * rows
    place = place.reshape(1)

    def ring_perm(value, step):
        pairs = [
            (r + i, r + (i + step) % RING) for r in range(0, count, RING) for i in range(RING)
        ]
        return lax.ppermute(value, "seq", pairs)

    def exchange(pieces):
        return [pieces[0]] + [ring_perm(pieces[d], d) for d in range(1, RING)]

    def ahead(value, step):
        return lax.ppermute(value, "seq", [(i, i + step) for i in range(count - step)])

    wide = conv_in.astype(jnp.float32)
    energy = lax.psum(jnp.sum(wide * wide, axis=1), "ch")
    rms = lax.rsqrt(energy / CONV_CH + 1e-06)
    rms_wide = jnp.broadcast_to(rms[:, None], (rows, 128))
    last = (
        conv_in[rows - TAPS :].astype(jnp.float32)
        * rms[rows - TAPS :, None]
        * norm_gain[None, :]
    ).astype(jnp.bfloat16)
    tail = ahead(last, 1)
    query_out, key_out = quarters(place, queries, keys)
    key_in = exchange(key_out)

    positions = ring_base + jnp.arange(rows * RING, dtype=jnp.int32)
    begin_ring = begin_of(doc_lengths, positions)
    begin_att = jnp.broadcast_to(
        (begin_ring - ring_base)[:, None], (rows * RING, 128)
    )
    begin_own = begin_of(doc_lengths, base + jnp.arange(rows, dtype=jnp.int32)) - base
    begin_conv = jnp.broadcast_to(begin_own[:, None], (rows, 128))

    taps = filters[:, ::-1].astype(jnp.float32)
    rest, part, bands = convolve_own(
        place, conv_in, rms_wide, norm_gain[None, :], taps, gate, begin_conv
    )
    mixed, value_out = convolve_tail(place, tail, part, bands, rest, gate)
    key_in, mixed = lax.optimization_barrier((key_in, mixed))
    key_halo = ahead(last_shards(place, key_in, 1)[0], RING)
    value_in = exchange(value_out)
    late = last_shards(place, value_in, CUTS)
    late, query_out = lax.optimization_barrier((late, query_out))
    query_in = exchange(query_out)
    value_halo = ahead(late[0], RING)
    *sums, query_all = attend_ring(place, begin_att, query_in, key_in, value_in)
    pieces = attend_halo(place, begin_att, sums, query_all, key_halo, value_halo)
    attended = whole_width(place, [exchange(pieces)])
    return (mixed, attended)


def solution(mesh):
    placed = (
        P("seq", "ch"),
        P("ch"),
        P("ch", None),
        P("seq", "ch"),
        P("seq", "ch"),
        P("seq", "ch"),
        P(),
    )
    return jax.shard_map(
        shards,
        mesh=mesh,
        in_specs=placed,
        out_specs=(P("seq", "ch"), P("seq", "ch")),
        check_vma=False,
    )
```

time: 107 us -> 100 us (0.935)
  waiting for transfers between devices: 49.6 us -> 36.3 us
  Pallas kernels: 18.9 us -> 26.1 us
  local copies, waits for them, and re-layouts: 5.6 us -> 2.53 us
  starting transfers between devices: 25.1 us -> 26.2 us
    ppermute x3, waiting for transfers between devices: 20.1 us -> 7.28 us  [ahead(): lax.ppermute(value, 'seq', [(i, i + step) for i in range(count - step)])]
    pallas_call x5 -> x7, Pallas kernels: 17.7 us -> 24.9 us  [the longest x1 6.55 us: attend_ring(): pl.pallas_call(kernel, out_shape=[jax.ShapeDtypeStruct((span, part), jnp....]
    ppermute x3, starting transfers between devices: 7.23 us -> 10.4 us  [ahead(): lax.ppermute(value, 'seq', [(i, i + step) for i in range(count - step)])]
    unnamed x22 -> x24, local copies, waits for them, and re-layouts: 5.05 us -> 1.97 us
    ppermute x12, starting transfers between devices: 17.8 us -> 15.8 us  [ring_perm(): return lax.ppermute(value, 'seq', pairs)]
  transfers between devices with their start and end apart: 15 -> 15, of which waited for: 8 -> 9; matrix products, arithmetic and copies ran while one was open for 1% -> 1% of each run, Pallas kernels for 7% -> 20%
where the time goes in v2:
time: 100 us; the launch traced here: 98.9 us
  waiting for transfers between devices  36.3 us (36%)
  starting transfers between devices  26.2 us (26%)
  Pallas kernels  26.1 us (26%)
  other arithmetic  4.07 us (4%)
  blocking collectives  2.6 us (3%)
  local copies, waits for them, and re-layouts  2.53 us (3%)
  between operations  1.1 us (1%)
    ppermute x12, waiting for transfers between devices, ring_perm(): return lax.ppermute(value, 'seq', pairs)  29 us
    ppermute x12, starting transfers between devices, ring_perm(): return lax.ppermute(value, 'seq', pairs)  15.8 us
    ppermute x3, starting transfers between devices, ahead(): lax.ppermute(value, 'seq', [(i, i + step) for i in range(count - step)])  10.4 us
    ppermute x3, waiting for transfers between devices, ahead(): lax.ppermute(value, 'seq', [(i, i + step) for i in range(count - step)])  7.28 us
    pallas_call x1, Pallas kernels, attend_ring(): pl.pallas_call(kernel, out_shape=[jax.ShapeDtypeStruct((span, part), jnp....  6.55 us
    pallas_call x1, Pallas kernels, convolve_own(): pl.pallas_call(kernel, out_shape=[jax.ShapeDtypeStruct((rows - TAPS, widt...  6.27 us
    pallas_call x1, Pallas kernels, attend_halo(): pl.pallas_call(kernel, out_shape=[jax.ShapeDtypeStruct((rows, part), jnp....  5.68 us
    pallas_call x1, Pallas kernels, convolve_tail(): pl.pallas_call(kernel, out_shape=[jax.ShapeDtypeStruct((rows, width), jnp...  3.39 us
  transfers between devices with their start and end apart: 15, of which 9 were waited for; matrix products, arithmetic and copies ran while one was open for 1% of the time, Pallas kernels for 20%

profile of v2, /device:TPU:128, one launch (start us, length us, event | category | flops | bytes accessed | tf_op | source)
XLA Modules:
  0.0 98.9 jit_solution(1650091600263870197)
XLA Ops:
  0.6 0.0 copy-start.2
  0.6 0.0 copy-start.11
  0.6 1.6 %multiply_reduce_fusion = f32[256]{0:T(256)S(1)} fusion(bf16[256,2048]{1,0:T(8,128)(2,1)} %x_ref.1), kind=kLoop, calls=%fused_computation | loop fusion | flops 1572608 | bytes 1049600 | tf_op jit(solution)/shard_map/reduce_sum | solution.py:407
  2.3 0.0 copy-start.1
  2.3 2.6 %psum.7 = f32[256]{0:T(256)S(1)} all-reduce(f32[256]{0:T(256)S(1)} %multiply_reduce_fusion), channel_id=1, replica_groups=mesh['seq'=128,'ch'=2] {'ch'}, use_global_device_ids=true, to_apply=%region_1.0 | all-reduce | flops 256 | bytes 2048 | tf_op jit(solution)/shard_map/psum | solution.py:407
  4.9 2.0 %multiply_convert_fusion = bf16[128,2048]{1,0:T(8,128)(2,1)} fusion(f32[2048]{0:T(1024)} %param.8, f32[128]{0:T(128)S(1)} %slice.7, bf16[256,2048]{1,0:T(8,128)(2,1)} %x_ref.1), kind=kLoop, calls=%fused_computation.1 | loop fusion | flops 1048576 | bytes 1057280 | tf_op jit(solution)/shard_map/convert_element_type | solution.py:414
  6.9 3.4 %collective-permute-start.3 = (bf16[128,2048]{1,0:T(8,128)(2,1)}, bf16[128,2048]{1,0:T(8,128)(2,1)}, u32[]{:S(2)}, u32[]{:S(2)}) collective-permute-start(bf16[128,2048]{1,0:T(8,128)(2,1)} %multiply_convert_fusion), channel_id=1, source_target_pairs={{0,2},{2,4},{4,6},{6,8},{8,10},{10,12},{12,14},{14,16},{16,18},{18... | collective-permute-start | bytes 1572872 | tf_op jit(solution)/shard_map/ppermute | solution.py:404
  10.3 0.0 copy-done.2
  10.3 0.0 copy-start.3
  10.4 1.2 %copy-done.3 = bf16[256,2048]{1,0:T(8,128)(2,1)S(1)} copy-done((bf16[256,2048]{1,0:T(8,128)(2,1)S(1)}, bf16[256,2048]{1,0:T(8,128)(2,1)}, u32[]{:S(2)}) %copy-start.3) | copy-done | bytes 1048600
  11.6 1.2 %quarters.1 = (bf16[256,512]{1,0:T(8,128)(2,1)S(1)}, bf16[256,512]{1,0:T(8,128)(2,1)S(1)}, bf16[256,512]{1,0:T(8,128)(2,1)S(1)}, bf16[256,512]{1,0:T(8,128)(2,1)...) custom-call(s32[1]{0:T(128)} %bitcast.place_ref, ...), custom_call_target="tpu_custom_call" | custom-call | tf_op jit(solution)/shard_map/quarters/pallas_call | solution.py:54
  12.7 0.0 copy-start.4
  12.8 0.7 copy-done.4
  13.5 1.5 %collective-permute-start = (bf16[256,512]{1,0:T(8,128)(2,1)}, bf16[256,512]{1,0:T(8,128)(2,1)S(1)}, u32[]{:S(2)}, u32[]{:S(2)}) collective-permute-start(bf16[256,512]{1,0:T(8,128)(2,1)} %get-tuple-element.37), channel_id=1, source_target_pairs={{0,2},{2,4},{4,6},{6,0},{8,10},{10,12},{12,14},{14,8},{16,18},{18,... | collective-permute-start | bytes 786440 | tf_op jit(solution)/shard_map/ppermute | solution.py:398
  15.0 2.7 %collective-permute-start.1 = (bf16[256,512]{1,0:T(8,128)(2,1)}, bf16[256,512]{1,0:T(8,128)(2,1)S(1)}, u32[]{:S(2)}, u32[]{:S(2)}) collective-permute-start(bf16[256,512]{1,0:T(8,128)(2,1)} %get-tuple-element.38), channel_id=1, source_target_pairs={{0,4},{2,6},{4,0},{6,2},{8,12},{10,14},{12,8},{14,10},{16,20},{18,... | collective-permute-start | bytes 786440 | tf_op jit(solution)/shard_map/ppermute | solution.py:398
  17.7 0.0 copy-done.7
  17.7 0.0 copy-done.8
  17.7 0.0 copy-done.9
  17.7 1.2 %collective-permute-start.2 = (bf16[256,512]{1,0:T(8,128)(2,1)}, bf16[256,512]{1,0:T(8,128)(2,1)S(1)}, u32[]{:S(2)}, u32[]{:S(2)}) collective-permute-start(bf16[256,512]{1,0:T(8,128)(2,1)} %get-tuple-element.39), channel_id=1, source_target_pairs={{0,6},{2,0},{4,2},{6,4},{8,14},{10,8},{12,10},{14,12},{16,22},{18,... | collective-permute-start | bytes 786440 | tf_op jit(solution)/shard_map/ppermute | solution.py:398
  18.9 0.1 copy.11
  19.0 0.1 reduce-window.9
  19.1 0.1 reduce
  19.2 0.1 select_reduce_fusion.1
  19.3 0.1 rev.3
  19.4 0.1 broadcast_in_dim.24.rms_ref
  19.5 0.1 broadcast_in_dim.27.begin_ref
  19.6 0.0 copy-done
  19.7 0.0 copy-done.1
  19.7 0.0 copy-done.6
  19.7 6.3 %convolve_own.1 = (bf16[128,2048]{1,0:T(8,128)(2,1)S(1)}, f32[128,2048]{1,0:T(8,128)S(1)}, bf16[16,1024,128]{2,1,0:T(8,128)(2,1)S(1)}) custom-call(bf16[256,2048]{1,0:T(8,128)(2,1)S(1)} %copy-done, f32[256,128]{1,0:T(8,128)S(1)} %broadcast_in_dim.24.rms_ref, f32[1,2048]{1,0:T(1,128)S(1)} %bitcast.3, f32[128,128]{1,0:T(8,128)S(1)} %convert_element_type.15.taps_ref, ...), custom_call_target="tpu_custom_call" | custom-call | tf_op jit(solution)/shard_map/convolve_own/pallas_call | solution.py:191
  26.0 2.7 %collective-permute-done.3.tail_ref = bf16[128,2048]{1,0:T(8,128)(2,1)} collective-permute-done((bf16[128,2048]{1,0:T(8,128)(2,1)}, bf16[128,2048]{1,0:T(8,128)(2,1)}, u32[]{:S(2)}, u32[]{:S(2)}) %collective-permute-start.3) | collective-permute-done | bytes 524320 | tf_op jit(solution)/shard_map/ppermute | solution.py:404
  28.7 3.4 %convolve_tail.1 = (bf16[256,2048]{1,0:T(8,128)(2,1)}, bf16[256,512]{1,0:T(8,128)(2,1)S(1)}, bf16[256,512]{1,0:T(8,128)(2,1)S(1)}, bf16[256,512]{1,0:T(8,128)(2,1)S(1)}, bf16[256,512]{1,0:T(8,128)(2,1)S(1)}) custom-call(s32[1]{0:T(128)} %bitcast.place_ref, bf16[128,2048]{1,0:T(8,128)(2,1)} %collective-permute-done.3.tail_ref, ...), custom_call_target="tpu_custom_call" | custom-call | tf_op jit(solution)/shard_map/convolve_tail/pallas_call | solution.py:239
  32.0 0.0 collective-permute-start.4
  32.1 0.0 collective-permute-start.5
  32.1 0.0 collective-permute-done.refs_5_.refs_1_
  32.1 3.2 %collective-permute-start.6 = (bf16[256,512]{1,0:T(8,128)(2,1)S(1)}, bf16[256,512]{1,0:T(8,128)(2,1)S(1)}, u32[]{:S(2)}, u32[]{:S(2)}) collective-permute-start(bf16[256,512]{1,0:T(8,128)(2,1)S(1)} %get-tuple-element.48), channel_id=1, source_target_pairs={{0,6},{2,0},{4,2},{6,4},{8,14},{10,8},{12,10},{14,12},{16,22},{18,... | collective-permute-start | bytes 786440 | tf_op jit(solution)/shard_map/ppermute | solution.py:398
  35.3 1.9 %collective-permute-done.1.refs_6_.refs_2_ = bf16[256,512]{1,0:T(8,128)(2,1)S(1)} collective-permute-done((bf16[256,512]{1,0:T(8,128)(2,1)}, bf16[256,512]{1,0:T(8,128)(2,1)S(1)}, u32[]{:S(2)}, u32[]{:S(2)}) %collective-permute-start.1) | collective-permute-done | bytes 262176 | tf_op jit(solution)/shard_map/ppermute | solution.py:398
  37.2 0.0 collective-permute-done.2.refs_7_.refs_3_
  37.2 1.0 last_shards.3
  38.2 3.5 %collective-permute-start.10 = (bf16[768,512]{1,0:T(8,128)(2,1)}, bf16[768,512]{1,0:T(8,128)(2,1)S(1)}, u32[]{:S(2)}, u32[]{:S(2)}) collective-permute-start(bf16[768,512]{1,0:T(8,128)(2,1)} %last_shards.3), channel_id=1, source_target_pairs={{0,8},{2,10},{4,12},{6,14},{8,16},{10,18},{12,20},{14,22},{16,24},... | collective-permute-start | bytes 2359304 | tf_op jit(solution)/shard_map/ppermute | solution.py:404
  41.8 1.1 %collective-permute-done.4.refs_1_.refs_9_ = bf16[256,512]{1,0:T(8,128)(2,1)S(1)} collective-permute-done((bf16[256,512]{1,0:T(8,128)(2,1)S(1)}, bf16[256,512]{1,0:T(8,128)(2,1)S(1)}, u32[]{:S(2)}, u32[]{:S(2)}) %collective-permute-start.4) | collective-permute-done | bytes 262176 | tf_op jit(solution)/shard_map/ppermute | solution.py:398
  42.9 4.8 %collective-permute-done.5.refs_2_.refs_10_ = bf16[256,512]{1,0:T(8,128)(2,1)S(1)} collective-permute-done((bf16[256,512]{1,0:T(8,128)(2,1)S(1)}, bf16[256,512]{1,0:T(8,128)(2,1)S(1)}, u32[]{:S(2)}, u32[]{:S(2)}) %collective-permute-start.5) | collective-permute-done | bytes 262176 | tf_op jit(solution)/shard_map/ppermute | solution.py:398
  47.7 0.0 collective-permute-done.6.refs_3_.refs_11_
  47.7 1.0 %last_shards.2 = bf16[768,512]{1,0:T(8,128)(2,1)} custom-call(s32[1]{0:T(128)} %bitcast.place_ref, bf16[256,512]{1,0:T(8,128)(2,1)S(1)} %get-tuple-element.45.refs_0_.refs_8_, bf16[256,512]{1,0:T(8,128)(2,1)S(1)} %collective-permute-done.4.refs_1_.refs_9_, bf16[256,512]{1,0:T(8,128)(2,1)S(1)} %collective-permute-done.5.refs_2_.refs_10_, ...), custom_call_target="tpu_custom_call" | custom-call | tf_op jit(solution)/shard_map/last_shards/pallas_call | solution.py:123
  48.7 3.5 %collective-permute-start.11 = (bf16[768,512]{1,0:T(8,128)(2,1)}, bf16[768,512]{1,0:T(8,128)(2,1)}, u32[]{:S(2)}, u32[]{:S(2)}) collective-permute-start(bf16[768,512]{1,0:T(8,128)(2,1)} %last_shards.2), channel_id=1, source_target_pairs={{0,8},{2,10},{4,12},{6,14},{8,16},{10,18},{12,20},{14,22},{16,24},... | collective-permute-start | bytes 2359304 | tf_op jit(solution)/shard_map/ppermute | solution.py:404
  52.3 0.1 collective-permute-start.7
  52.4 1.5 %collective-permute-start.8 = (bf16[256,512]{1,0:T(8,128)(2,1)}, bf16[256,512]{1,0:T(8,128)(2,1)S(1)}, u32[]{:S(2)}, u32[]{:S(2)}) collective-permute-start(bf16[256,512]{1,0:T(8,128)(2,1)} %copy-done.8), channel_id=1, source_target_pairs={{0,4},{2,6},{4,0},{6,2},{8,12},{10,14},{12,8},{14,10},{16,20},{18,... | collective-permute-start | bytes 786440 | tf_op jit(solution)/shard_map/ppermute | solution.py:398
  53.9 1.9 %collective-permute-start.9 = (bf16[256,512]{1,0:T(8,128)(2,1)}, bf16[256,512]{1,0:T(8,128)(2,1)S(1)}, u32[]{:S(2)}, u32[]{:S(2)}) collective-permute-start(bf16[256,512]{1,0:T(8,128)(2,1)} %copy-done.7), channel_id=1, source_target_pairs={{0,6},{2,0},{4,2},{6,4},{8,14},{10,8},{12,10},{14,12},{16,22},{18,... | collective-permute-start | bytes 786440 | tf_op jit(solution)/shard_map/ppermute | solution.py:398
  55.8 0.1 select_reduce_fusion
  55.9 10.7 %collective-permute-done.7.refs_1_ = bf16[256,512]{1,0:T(8,128)(2,1)S(1)} collective-permute-done((bf16[256,512]{1,0:T(8,128)(2,1)}, bf16[256,512]{1,0:T(8,128)(2,1)S(1)}, u32[]{:S(2)}, u32[]{:S(2)}) %collective-permute-start.7) | collective-permute-done | bytes 262176 | tf_op jit(solution)/shard_map/ppermute | solution.py:398
  66.7 0.0 collective-permute-done.8.refs_2_
  66.7 0.6 collective-permute-done.9.refs_3_
  67.3 0.2 broadcast_in_dim.33.begin_ref
  67.5 6.5 %attend_ring.1 = (f32[1024,512]{1,0:T(8,128)S(1)}, f32[1024,512]{1,0:T(8,128)S(1)}, f32[1024,512]{1,0:T(8,128)S(1)}, bf16[1024,512]{1,0:T(8,128)(2,1)S(1)}) custom-call(s32[1]{0:T(128)} %bitcast.place_ref, s32[1024,128]{1,0:T(8,128)S(1)} %broadcast_in_dim.33.begin_ref, bf16[256,512]{1,0:T(8,128)(2,1)S(1)} %copy-done.5, ...), custom_call_target="tpu_custom_call" | custom-call | tf_op jit(solution)/shard_map/attend_ring/pallas_call | solution.py:306
  74.0 0.0 collective-permute-done.10.k_ref
  74.0 4.6 %collective-permute-done.11.v_ref = bf16[768,512]{1,0:T(8,128)(2,1)} collective-permute-done((bf16[768,512]{1,0:T(8,128)(2,1)}, bf16[768,512]{1,0:T(8,128)(2,1)}, u32[]{:S(2)}, u32[]{:S(2)}) %collective-permute-start.11) | collective-permute-done | bytes 786464 | tf_op jit(solution)/shard_map/ppermute | solution.py:404
  78.6 5.7 %attend_halo.1 = (bf16[256,512]{1,0:T(8,128)(2,1)S(1)}, bf16[256,512]{1,0:T(8,128)(2,1)S(1)}, bf16[256,512]{1,0:T(8,128)(2,1)S(1)}, bf16[256,512]{1,0:T(8,128)(2,1)S(1)}) custom-call(s32[1]{0:T(128)} %bitcast.place_ref, s32[1024,128]{1,0:T(8,128)S(1)} %broadcast_in_dim.33.begin_ref, f32[1024,512]{1,0:T(8,128)S(1)} %get-tuple-element.61.acc_ref, ...), custom_call_target="tpu_custom_call" | custom-call | tf_op jit(solution)/shard_map/attend_halo/pallas_call | solution.py:371
  84.3 0.1 collective-permute-start.12
  84.4 1.0 collective-permute-start.13
  85.4 2.5 %collective-permute-start.14 = (bf16[256,512]{1,0:T(8,128)(2,1)S(1)}, bf16[256,512]{1,0:T(8,128)(2,1)S(1)}, u32[]{:S(2)}, u32[]{:S(2)}) collective-permute-start(bf16[256,512]{1,0:T(8,128)(2,1)S(1)} %get-tuple-element.69), channel_id=1, source_target_pairs={{0,6},{2,0},{4,2},{6,4},{8,14},{10,8},{12,10},{14,12},{16,22},{18,... | collective-permute-start | bytes 786440 | tf_op jit(solution)/shard_map/ppermute | solution.py:398
  87.9 9.2 %collective-permute-done.12.refs_1_ = bf16[256,512]{1,0:T(8,128)(2,1)S(1)} collective-permute-done((bf16[256,512]{1,0:T(8,128)(2,1)S(1)}, bf16[256,512]{1,0:T(8,128)(2,1)S(1)}, u32[]{:S(2)}, u32[]{:S(2)}) %collective-permute-start.12) | collective-permute-done | bytes 262176 | tf_op jit(solution)/shard_map/ppermute | solution.py:398
  97.1 0.0 collective-permute-done.13.refs_2_
  97.1 0.6 collective-permute-done.14.refs_3_
  97.7 1.0 %whole_width.1 = bf16[256,2048]{1,0:T(8,128)(2,1)} custom-call(s32[1]{0:T(128)} %bitcast.place_ref, bf16[256,512]{1,0:T(8,128)(2,1)S(1)} %get-tuple-element.66.refs_0_, bf16[256,512]{1,0:T(8,128)(2,1)S(1)} %collective-permute-done.12.refs_1_, bf16[256,512]{1,0:T(8,128)(2,1)S(1)} %collective-permute-done.13.refs_2_, ...), custom_call_target="tpu_custom_call" | custom-call | tf_op jit(solution)/shard_map/whole_width/pallas_call | solution.py:87
  (18 shorter events, 0.1 us)
Async XLA Ops:
  0.6 9.7 %copy-start.2 = (bf16[256,2048]{1,0:T(8,128)(2,1)S(1)}, bf16[256,2048]{1,0:T(8,128)(2,1)}, u32[]{:S(2)}) copy-start(bf16[256,2048]{1,0:T(8,128)(2,1)} %refs_0_.1) | copy-start | bytes 3145732
  0.6 18.3 %copy-start.11 = (s32[48]{0:T(128)S(1)}, s32[48]{0:T(128)}, u32[]{:S(2)}) copy-start(s32[48]{0:T(128)} %param.13) | copy-start | bytes 580
  2.2 17.4 %copy-start = (bf16[256,2048]{1,0:T(8,128)(2,1)S(1)}, bf16[256,2048]{1,0:T(8,128)(2,1)}, u32[]{:S(2)}) copy-start(bf16[256,2048]{1,0:T(8,128)(2,1)} %x_ref.1) | copy-start | bytes 3145732
  2.3 17.4 %copy-start.1 = (bf16[256,2048]{1,0:T(8,128)(2,1)S(1)}, bf16[256,2048]{1,0:T(8,128)(2,1)}, u32[]{:S(2)}) copy-start(bf16[256,2048]{1,0:T(8,128)(2,1)} %gate_ref.3) | copy-start | bytes 3145732
  6.9 21.7 %collective-permute-start.3 = (bf16[128,2048]{1,0:T(8,128)(2,1)}, bf16[128,2048]{1,0:T(8,128)(2,1)}, u32[]{:S(2)}, u32[]{:S(2)}) collective-permute-start(bf16[128,2048]{1,0:T(8,128)(2,1)} %multiply_convert_fusion), channel_id=1, source_target_pairs={{0,2},{2,4},{4,6},{6,8},{8,10},{10,12},{12,14},{14,16},{16,18},{18... | collective-permute-start | bytes 1572872 | tf_op jit(solution)/shard_map/ppermute | solution.py:404
  10.3 1.2 %copy-start.3 = (bf16[256,2048]{1,0:T(8,128)(2,1)S(1)}, bf16[256,2048]{1,0:T(8,128)(2,1)}, u32[]{:S(2)}) copy-start(bf16[256,2048]{1,0:T(8,128)(2,1)} %refs_1_.1) | copy-start | bytes 3145732
  11.6 7.7 %copy-start.10 = (bf16[128,128]{1,0:T(8,128)(2,1)S(1)}, bf16[128,128]{1,0:T(8,128)(2,1)}, u32[]{:S(2)}) copy-start(bf16[128,128]{1,0:T(8,128)(2,1)} %param.9) | copy-start | bytes 98308
  11.6 8.1 %copy-start.6 = (f32[2048]{0:T(1024)S(1)}, f32[2048]{0:T(1024)}, u32[]{:S(2)}) copy-start(f32[2048]{0:T(1024)} %param.8) | copy-start | bytes 24580
  12.7 0.7 copy-start.4
  13.5 4.2 %copy-start.7 = (bf16[256,512]{1,0:T(8,128)(2,1)}, bf16[256,512]{1,0:T(8,128)(2,1)S(1)}, u32[]{:S(2)}) copy-start(bf16[256,512]{1,0:T(8,128)(2,1)S(1)} %get-tuple-element.56) | copy-start | bytes 786436
  13.5 4.2 %copy-start.8 = (bf16[256,512]{1,0:T(8,128)(2,1)}, bf16[256,512]{1,0:T(8,128)(2,1)S(1)}, u32[]{:S(2)}) copy-start(bf16[256,512]{1,0:T(8,128)(2,1)S(1)} %get-tuple-element.55) | copy-start | bytes 786436
  13.5 4.2 %copy-start.9 = (bf16[256,512]{1,0:T(8,128)(2,1)}, bf16[256,512]{1,0:T(8,128)(2,1)S(1)}, u32[]{:S(2)}) copy-start(bf16[256,512]{1,0:T(8,128)(2,1)S(1)} %get-tuple-element.54) | copy-start | bytes 786436
  13.5 18.6 %collective-permute-start = (bf16[256,512]{1,0:T(8,128)(2,1)}, bf16[256,512]{1,0:T(8,128)(2,1)S(1)}, u32[]{:S(2)}, u32[]{:S(2)}) collective-permute-start(bf16[256,512]{1,0:T(8,128)(2,1)} %get-tuple-element.37), channel_id=1, source_target_pairs={{0,2},{2,4},{4,6},{6,0},{8,10},{10,12},{12,14},{14,8},{16,18},{18,... | collective-permute-start | bytes 786440 | tf_op jit(solution)/shard_map/ppermute | solution.py:398
  15.0 22.3 %collective-permute-start.1 = (bf16[256,512]{1,0:T(8,128)(2,1)}, bf16[256,512]{1,0:T(8,128)(2,1)S(1)}, u32[]{:S(2)}, u32[]{:S(2)}) collective-permute-start(bf16[256,512]{1,0:T(8,128)(2,1)} %get-tuple-element.38), channel_id=1, source_target_pairs={{0,4},{2,6},{4,0},{6,2},{8,12},{10,14},{12,8},{14,10},{16,20},{18,... | collective-permute-start | bytes 786440 | tf_op jit(solution)/shard_map/ppermute | solution.py:398
  17.7 19.5 %collective-permute-start.2 = (bf16[256,512]{1,0:T(8,128)(2,1)}, bf16[256,512]{1,0:T(8,128)(2,1)S(1)}, u32[]{:S(2)}, u32[]{:S(2)}) collective-permute-start(bf16[256,512]{1,0:T(8,128)(2,1)} %get-tuple-element.39), channel_id=1, source_target_pairs={{0,6},{2,0},{4,2},{6,4},{8,14},{10,8},{12,10},{14,12},{16,22},{18,... | collective-permute-start | bytes 786440 | tf_op jit(solution)/shard_map/ppermute | solution.py:398
  32.0 10.8 %collective-permute-start.4 = (bf16[256,512]{1,0:T(8,128)(2,1)S(1)}, bf16[256,512]{1,0:T(8,128)(2,1)S(1)}, u32[]{:S(2)}, u32[]{:S(2)}) collective-permute-start(bf16[256,512]{1,0:T(8,128)(2,1)S(1)} %get-tuple-element.46), channel_id=1, source_target_pairs={{0,2},{2,4},{4,6},{6,0},{8,10},{10,12},{12,14},{14,8},{16,18},{18,... | collective-permute-start | bytes 786440 | tf_op jit(solution)/shard_map/ppermute | solution.py:398
  32.1 15.7 %collective-permute-start.5 = (bf16[256,512]{1,0:T(8,128)(2,1)S(1)}, bf16[256,512]{1,0:T(8,128)(2,1)S(1)}, u32[]{:S(2)}, u32[]{:S(2)}) collective-permute-start(bf16[256,512]{1,0:T(8,128)(2,1)S(1)} %get-tuple-element.47), channel_id=1, source_target_pairs={{0,4},{2,6},{4,0},{6,2},{8,12},{10,14},{12,8},{14,10},{16,20},{18,... | collective-permute-start | bytes 786440 | tf_op jit(solution)/shard_map/ppermute | solution.py:398
  32.1 15.7 %collective-permute-start.6 = (bf16[256,512]{1,0:T(8,128)(2,1)S(1)}, bf16[256,512]{1,0:T(8,128)(2,1)S(1)}, u32[]{:S(2)}, u32[]{:S(2)}) collective-permute-start(bf16[256,512]{1,0:T(8,128)(2,1)S(1)} %get-tuple-element.48), channel_id=1, source_target_pairs={{0,6},{2,0},{4,2},{6,4},{8,14},{10,8},{12,10},{14,12},{16,22},{18,... | collective-permute-start | bytes 786440 | tf_op jit(solution)/shard_map/ppermute | solution.py:398
  37.2 30.2 %copy-start.5 = (bf16[256,512]{1,0:T(8,128)(2,1)S(1)}, bf16[256,512]{1,0:T(8,128)(2,1)}, u32[]{:S(2)}) copy-start(bf16[256,512]{1,0:T(8,128)(2,1)} %copy-done.4) | copy-start | bytes 786436
  38.2 35.8 %collective-permute-start.10 = (bf16[768,512]{1,0:T(8,128)(2,1)}, bf16[768,512]{1,0:T(8,128)(2,1)S(1)}, u32[]{:S(2)}, u32[]{:S(2)}) collective-permute-start(bf16[768,512]{1,0:T(8,128)(2,1)} %last_shards.3), channel_id=1, source_target_pairs={{0,8},{2,10},{4,12},{6,14},{8,16},{10,18},{12,20},{14,22},{16,24},... | collective-permute-start | bytes 2359304 | tf_op jit(solution)/shard_map/ppermute | solution.py:404
  48.7 29.9 %collective-permute-start.11 = (bf16[768,512]{1,0:T(8,128)(2,1)}, bf16[768,512]{1,0:T(8,128)(2,1)}, u32[]{:S(2)}, u32[]{:S(2)}) collective-permute-start(bf16[768,512]{1,0:T(8,128)(2,1)} %last_shards.2), channel_id=1, source_target_pairs={{0,8},{2,10},{4,12},{6,14},{8,16},{10,18},{12,20},{14,22},{16,24},... | collective-permute-start | bytes 2359304 | tf_op jit(solution)/shard_map/ppermute | solution.py:404
  52.3 14.4 %collective-permute-start.7 = (bf16[256,512]{1,0:T(8,128)(2,1)}, bf16[256,512]{1,0:T(8,128)(2,1)S(1)}, u32[]{:S(2)}, u32[]{:S(2)}) collective-permute-start(bf16[256,512]{1,0:T(8,128)(2,1)} %copy-done.9), channel_id=1, source_target_pairs={{0,2},{2,4},{4,6},{6,0},{8,10},{10,12},{12,14},{14,8},{16,18},{18,... | collective-permute-start | bytes 786440 | tf_op jit(solution)/shard_map/ppermute | solution.py:398
  52.4 14.3 %collective-permute-start.8 = (bf16[256,512]{1,0:T(8,128)(2,1)}, bf16[256,512]{1,0:T(8,128)(2,1)S(1)}, u32[]{:S(2)}, u32[]{:S(2)}) collective-permute-start(bf16[256,512]{1,0:T(8,128)(2,1)} %copy-done.8), channel_id=1, source_target_pairs={{0,4},{2,6},{4,0},{6,2},{8,12},{10,14},{12,8},{14,10},{16,20},{18,... | collective-permute-start | bytes 786440 | tf_op jit(solution)/shard_map/ppermute | solution.py:398
  53.9 13.4 %collective-permute-start.9 = (bf16[256,512]{1,0:T(8,128)(2,1)}, bf16[256,512]{1,0:T(8,128)(2,1)S(1)}, u32[]{:S(2)}, u32[]{:S(2)}) collective-permute-start(bf16[256,512]{1,0:T(8,128)(2,1)} %copy-done.7), channel_id=1, source_target_pairs={{0,6},{2,0},{4,2},{6,4},{8,14},{10,8},{12,10},{14,12},{16,22},{18,... | collective-permute-start | bytes 786440 | tf_op jit(solution)/shard_map/ppermute | solution.py:398
  84.3 12.8 %collective-permute-start.12 = (bf16[256,512]{1,0:T(8,128)(2,1)S(1)}, bf16[256,512]{1,0:T(8,128)(2,1)S(1)}, u32[]{:S(2)}, u32[]{:S(2)}) collective-permute-start(bf16[256,512]{1,0:T(8,128)(2,1)S(1)} %get-tuple-element.67), channel_id=1, source_target_pairs={{0,2},{2,4},{4,6},{6,0},{8,10},{10,12},{12,14},{14,8},{16,18},{18,... | collective-permute-start | bytes 786440 | tf_op jit(solution)/shard_map/ppermute | solution.py:398
  84.4 12.7 %collective-permute-start.13 = (bf16[256,512]{1,0:T(8,128)(2,1)S(1)}, bf16[256,512]{1,0:T(8,128)(2,1)S(1)}, u32[]{:S(2)}, u32[]{:S(2)}) collective-permute-start(bf16[256,512]{1,0:T(8,128)(2,1)S(1)} %get-tuple-element.68), channel_id=1, source_target_pairs={{0,4},{2,6},{4,0},{6,2},{8,12},{10,14},{12,8},{14,10},{16,20},{18,... | collective-permute-start | bytes 786440 | tf_op jit(solution)/shard_map/ppermute | solution.py:398
  85.4 12.3 %collective-permute-start.14 = (bf16[256,512]{1,0:T(8,128)(2,1)S(1)}, bf16[256,512]{1,0:T(8,128)(2,1)S(1)}, u32[]{:S(2)}, u32[]{:S(2)}) collective-permute-start(bf16[256,512]{1,0:T(8,128)(2,1)S(1)} %get-tuple-element.69), channel_id=1, source_target_pairs={{0,6},{2,0},{4,2},{6,4},{8,14},{10,8},{12,10},{14,12},{16,22},{18,... | collective-permute-start | bytes 786440 | tf_op jit(solution)/shard_map/ppermute | solution.py:398

commit v3 on v2

--- a/solution.py
+++ b/solution.py
@@ -16,13 +16,6 @@
 SMEM = pl.BlockSpec(memory_space=pltpu.SMEM)
 VMEM = pl.BlockSpec(memory_space=pltpu.VMEM)
 NEG = -1e30
-
-
-def begin_of(doc_lengths, positions):
-    ends = jnp.cumsum(doc_lengths)
-    starts = ends - doc_lengths
-    inside = starts[None, :] <= positions[:, None]
-    return jnp.max(jnp.where(inside, starts[None, :], 0), axis=1)
 
 
 def params(mib):
@@ -133,24 +126,136 @@
     )(place, *pieces)
 
 
-def convolve_own(place, conv_in, rms, gain, taps, gate, begin):
+def lead_in(conv_in, gain):
+    rows, width = conv_in.shape
+    step = 128
+    parts = rows // step
+
+    def kernel(x_hbm, gain_in, x_ref, energy_ref, gain_ref, sem):
+        gain_ref[...] = gain_in[...]
+        copies = [
+            pltpu.make_async_copy(
+                x_hbm.at[pl.ds(p * step, step), :], x_ref.at[pl.ds(p * step, step), :], sem.at[p]
+            )
+            for p in range(parts)
+        ]
+        for copy in copies:
+            copy.start()
+        for p in range(parts):
+            copies[p].wait()
+            here = slice(p * step, (p + 1) * step)
+            total = jnp.zeros((step, 128), jnp.float32)
+            for at in range(0, width, 128):
+                wide = x_ref[here, at : at + 128].astype(jnp.float32)
+                total = total + wide * wide
+            energy_ref[p : p + 1, :] = jnp.sum(total.T, axis=0, keepdims=True)
+
+    return pl.pallas_call(
+        kernel,
+        out_shape=[
+            jax.ShapeDtypeStruct((rows, width), conv_in.dtype),
+            jax.ShapeDtypeStruct((parts, step), jnp.float32),
+            jax.ShapeDtypeStruct(gain.shape, jnp.float32),
+        ],
+        in_specs=[HBM, VMEM],
+        out_specs=[VMEM] * 3,
+        scratch_shapes=[pltpu.SemaphoreType.DMA((parts,))],
+        compiler_params=params(8),
+        name="lead_in",
+    )(conv_in, gain)
+
+
+def as_column(line):
+    return jnp.broadcast_to(line, (128, 128)).T
+
+
+def norm_last(conv_in, energy, gain):
+    rows, width = conv_in.shape
+
+    def kernel(x_ref, energy_ref, gain_ref, out_ref):
+        rms = lax.rsqrt(as_column(energy_ref[rows // 128 - 1 :, :]) / CONV_CH + 1e-06)
+        for at in range(0, width, 128):
+            cols = slice(at, at + 128)
+            out_ref[:, cols] = (
+                x_ref[rows - TAPS :, cols].astype(jnp.float32) * rms * gain_ref[:, cols]
+            ).astype(jnp.bfloat16)
+
+    return pl.pallas_call(
+        kernel,
+        out_shape=jax.ShapeDtypeStruct((TAPS, width), jnp.bfloat16),
+        in_specs=[VMEM] * 3,
+        out_specs=VMEM,
+        compiler_params=params(8),
+        name="norm_last",
+    )(conv_in, energy, gain)
+
+
+def begin_from(lengths_ref, base, rows):
+    position = lax.broadcasted_iota(jnp.int32, (8, 128), 0) * 128
+    position = position + lax.broadcasted_iota(jnp.int32, (8, 128), 1)
+    begin = jnp.full((8, 128), 0, jnp.int32) - base
+    start = 0 - base
+    for i in range(lengths_ref.shape[0] - 1):
+        start = start + lengths_ref[i]
+        begin = jnp.where(position >= start, start, begin)
+    return begin.astype(jnp.float32)
+
+
+def ring_begins(lengths, ring_base, rows):
+    def kernel(lengths_ref, base_ref, begin_ref, edge_ref):
+        base = base_ref[0]
+        lines = begin_from(lengths_ref, base, rows * RING)
+        for b in range(rows * RING // 128):
+            begin_ref[b * 128 : (b + 1) * 128, :] = as_column(lines[b : b + 1, :]).astype(
+                jnp.int32
+            )
+        for s in range(RING):
+            start = 0 - base
+            edge = start
+            for i in range(lengths_ref.shape[0] - 1):
+                start = start + lengths_ref[i]
+                edge = jnp.where(start <= s * rows, start, edge)
+            edge_ref[s] = edge
+
+    return pl.pallas_call(
+        kernel,
+        out_shape=[
+            jax.ShapeDtypeStruct((rows * RING, 128), jnp.int32),
+            jax.ShapeDtypeStruct((RING,), jnp.int32),
+        ],
+        in_specs=[SMEM] * 2,
+        out_specs=[VMEM, SMEM],
+        compiler_params=params(8),
+        name="ring_begins",
+    )(lengths, ring_base)
+
+
+def convolve_own(base, lengths, conv_in, energy, gain, filters, gate):
     rows, width = conv_in.shape
     lanes = 128
     per = lanes // GROUP
     blocks = rows // TAPS
 
-    def kernel(x_ref, rms_ref, gain_ref, taps_ref, gate_ref, begin_ref, *refs):
-        mixed_ref, part_ref, band_ref, masks, src, lhs = refs
+    def kernel(
+        base_ref, lengths_ref, x_ref, energy_ref, gain_ref, filter_ref, gate_ref, *refs
+    ):
+        mixed_ref, part_ref, band_ref, masks, src, lhs, rms_ref, taps_ref = refs
+        for b in range(rows // 128):
+            column = as_column(energy_ref[b : b + 1, :])
+            rms_ref[b * 128 : (b + 1) * 128, :] = lax.rsqrt(column / CONV_CH + 1e-06)
+        begin = begin_from(lengths_ref, base_ref[0], rows)
         out_row = lax.broadcasted_iota(jnp.int32, (TAPS, lanes), 0)
         src_col = lax.broadcasted_iota(jnp.int32, (TAPS, lanes), 1)
         for b in range(blocks):
-            first = begin_ref[b * TAPS : (b + 1) * TAPS, :]
+            first = as_column(begin[b : b + 1, :]).astype(jnp.int32)
             low = b * TAPS
             before = (src_col > out_row) & (src_col + (low - TAPS) >= first)
             inside = (src_col <= out_row) & (src_col + low >= first)
             masks[2 * b] = jnp.where(before, 1.0, 0.0).astype(jnp.bfloat16)
             masks[2 * b + 1] = jnp.where(inside, 1.0, 0.0).astype(jnp.bfloat16)
         lane_group = lax.broadcasted_iota(jnp.int32, (TAPS, lanes), 1) // GROUP
+        flip = jnp.where(src_col + out_row == TAPS - 1, 1.0, 0.0).astype(jnp.bfloat16)
+        taps_ref[...] = jnp.dot(filter_ref[...], flip, preferred_element_type=jnp.float32)
 
         def pick(full):
             picked = full[:TAPS]
@@ -195,16 +300,18 @@
             jax.ShapeDtypeStruct((TAPS, width), jnp.float32),
             jax.ShapeDtypeStruct((width // lanes, per * TAPS, lanes), jnp.bfloat16),
         ],
-        in_specs=[VMEM] * 6,
+        in_specs=[SMEM] * 2 + [VMEM] * 5,
         out_specs=[VMEM] * 3,
         scratch_shapes=[
             pltpu.VMEM((2 * blocks, TAPS, lanes), jnp.bfloat16),
             pltpu.VMEM((rows, lanes), jnp.bfloat16),
             pltpu.VMEM((blocks, per * TAPS, 2 * lanes), jnp.bfloat16),
+            pltpu.VMEM((rows, lanes), jnp.float32),
+            pltpu.VMEM(filters.shape, jnp.float32),
         ],
         compiler_params=params(20),
         name="convolve_own",
-    )(conv_in, rms, gain, taps, gate, begin)
+    )(base, lengths, conv_in, energy, gain, filters, gate)
 
 
 def convolve_tail(place, tail, part, bands, rest, gate):
@@ -284,14 +391,18 @@
                     valid = valid & (key + c * 128 <= row)
                 bias.append(jnp.where(valid, 0.0, NEG))
             bias = jnp.concatenate(bias, axis=1)
-            for h in range(heads):
-                cols = slice(h * HEAD_DIM, (h + 1) * HEAD_DIM)
-                score = bias + lax.dot_general(
-                    q_all[here, cols],
-                    k_all[:size, cols],
+            scores = [
+                lax.dot_general(
+                    q_all[here, h * HEAD_DIM : (h + 1) * HEAD_DIM],
+                    k_all[:size, h * HEAD_DIM : (h + 1) * HEAD_DIM],
                     BOTH_LAST,
                     preferred_element_type=jnp.float32,
                 )
+                for h in range(heads)
+            ]
+            for h in range(heads):
+                cols = slice(h * HEAD_DIM, (h + 1) * HEAD_DIM)
+                score = bias + scores[h]
                 top = jnp.max(score, axis=1, keepdims=True)
                 weight = jnp.exp2((score - top) * SCALE)
                 total = jnp.sum(weight, axis=1, keepdims=True)
@@ -319,38 +430,47 @@
     )(place, begin, *queries, *keys, *values)
 
 
-def attend_halo(place, begin, sums, queries, key_halo, value_halo):
+def attend_halo(place, edges, begin, sums, queries, key_halo, value_halo):
     back, part = value_halo.shape
     rows = back // (RING - 1)
     heads = part // HEAD_DIM
     span = RING * rows
 
-    def kernel(place_ref, begin_ref, acc_ref, top_ref, total_ref, q_ref, k_ref, v_ref, *refs):
+    def kernel(
+        place_ref, edge_ref, begin_ref, acc_ref, top_ref, total_ref, q_ref, k_ref, v_ref, *refs
+    ):
         outs, o_all, sem = refs[:RING], refs[RING], refs[RING + 1]
         place = place_ref[0]
-        for s in (3, 0, 1, 2):
+        def tile(s, blocks):
             here = slice(s * rows, (s + 1) * rows)
-            size = (RING - 1 - s) * rows
-            low = s * rows
+            low = back - blocks * rows
+            size = blocks * rows
             if size:
                 first = begin_ref[here, :]
-                key = lax.broadcasted_iota(jnp.int32, (rows, 128), 1) + (low - back)
+                key = lax.broadcasted_iota(jnp.int32, (rows, 128), 1) - size
                 bias = jnp.concatenate(
                     [jnp.where(key + c * 128 >= first, 0.0, NEG) for c in range(size // 128)],
                     axis=1,
                 )
+            scores = []
+            for h in range(heads):
+                cols = slice(h * HEAD_DIM, (h + 1) * HEAD_DIM)
+                if size:
+                    scores.append(
+                        lax.dot_general(
+                            q_ref[here, cols],
+                            k_ref[low:, cols],
+                            BOTH_LAST,
+                            preferred_element_type=jnp.float32,
+                        )
+                    )
             for h in range(heads):
                 cols = slice(h * HEAD_DIM, (h + 1) * HEAD_DIM)
                 top = top_ref[here, cols]
                 total = total_ref[here, cols]
                 out = acc_ref[here, cols]
                 if size:
-                    score = bias + lax.dot_general(
-                        q_ref[here, cols],
-                        k_ref[low:, cols],
-                        BOTH_LAST,
-                        preferred_element_type=jnp.float32,
-                    )
+                    score = bias + scores[h]
                     new_top = jnp.maximum(top, jnp.max(score, axis=1, keepdims=True))
                     wide_top = jnp.concatenate([new_top] * (size // HEAD_DIM), axis=1)
                     weight = jnp.exp2((score - wide_top) * SCALE)
@@ -362,6 +482,22 @@
                         preferred_element_type=jnp.float32,
                     )
                 o_all[here, cols] = (out * (1.0 / total)).astype(jnp.bfloat16)
+
+        for s in (3, 0, 1, 2):
+            here = slice(s * rows, (s + 1) * rows)
+            most = RING - 1 - s
+            if most == 0:
+                tile(s, 0)
+            need = -edge_ref[s]
+            for blocks in range(most + 1 if most else 0):
+                above = need > (blocks - 1) * rows
+                below = need <= blocks * rows
+                if blocks == 0:
+                    pl.when(below)(lambda s=s: tile(s, 0))
+                elif blocks == most:
+                    pl.when(above)(lambda s=s, blocks=blocks: tile(s, blocks))
+                else:
+                    pl.when(above & below)(lambda s=s, blocks=blocks: tile(s, blocks))
             for d in range(RING):
                 copy = pltpu.make_async_copy(o_all.at[here, :], outs[d], sem.at[d])
                 pl.when(lax.rem(place + d, RING) == s)(copy.start)
@@ -371,7 +507,7 @@
     return pl.pallas_call(
         kernel,
         out_shape=[jax.ShapeDtypeStruct((rows, part), jnp.bfloat16) for _ in range(RING)],
-        in_specs=[SMEM] + [VMEM] * 7,
+        in_specs=[SMEM, SMEM] + [VMEM] * 7,
         out_specs=[VMEM] * RING,
         scratch_shapes=[
             pltpu.VMEM((span, part), jnp.bfloat16),
@@ -379,7 +515,7 @@
         ],
         compiler_params=params(20),
         name="attend_halo",
-    )(place, begin, *sums, queries, key_halo, value_halo)
+    )(place, edges, begin, *sums, queries, key_halo, value_halo)
 
 
 def shards(conv_in, norm_gain, filters, gate, queries, keys, doc_lengths):
@@ -403,32 +539,19 @@
     def ahead(value, step):
         return lax.ppermute(value, "seq", [(i, i + step) for i in range(count - step)])
 
-    wide = conv_in.astype(jnp.float32)
-    energy = lax.psum(jnp.sum(wide * wide, axis=1), "ch")
-    rms = lax.rsqrt(energy / CONV_CH + 1e-06)
-    rms_wide = jnp.broadcast_to(rms[:, None], (rows, 128))
-    last = (
-        conv_in[rows - TAPS :].astype(jnp.float32)
-        * rms[rows - TAPS :, None]
-        * norm_gain[None, :]
-    ).astype(jnp.bfloat16)
-    tail = ahead(last, 1)
+    lead, energy, gain = lead_in(conv_in, norm_gain[None, :])
+    energy = lax.psum(energy, "ch")
+    tail = ahead(norm_last(lead, energy, gain), 1)
+    keys, queries, energy = lax.optimization_barrier((keys, queries, energy))
     query_out, key_out = quarters(place, queries, keys)
     key_in = exchange(key_out)
 
-    positions = ring_base + jnp.arange(rows * RING, dtype=jnp.int32)
-    begin_ring = begin_of(doc_lengths, positions)
-    begin_att = jnp.broadcast_to(
-        (begin_ring - ring_base)[:, None], (rows * RING, 128)
-    )
-    begin_own = begin_of(doc_lengths, base + jnp.arange(rows, dtype=jnp.int32)) - base
-    begin_conv = jnp.broadcast_to(begin_own[:, None], (rows, 128))
-
-    taps = filters[:, ::-1].astype(jnp.float32)
     rest, part, bands = convolve_own(
-        place, conv_in, rms_wide, norm_gain[None, :], taps, gate, begin_conv
+        base.reshape(1), doc_lengths, lead, energy, gain, filters, gate
     )
     mixed, value_out = convolve_tail(place, tail, part, bands, rest, gate)
+    lengths, mixed = lax.optimization_barrier((doc_lengths, mixed))
+    begin_att, edges = ring_begins(lengths, ring_base.reshape(1), rows)
     key_in, mixed = lax.optimization_barrier((key_in, mixed))
     key_halo = ahead(last_shards(place, key_in, 1)[0], RING)
     value_in = exchange(value_out)
@@ -437,7 +560,7 @@
     query_in = exchange(query_out)
     value_halo = ahead(late[0], RING)
     *sums, query_all = attend_ring(place, begin_att, query_in, key_in, value_in)
-    pieces = attend_halo(place, begin_att, sums, query_all, key_halo, value_halo)
+    pieces = attend_halo(place, edges, begin_att, sums, query_all, key_halo, value_halo)
     attended = whole_width(place, [exchange(pieces)])
     return (mixed, attended)
 

time: 100 us -> 98 us (0.980)
  other arithmetic: 4.07 us -> 0 us
  local copies, waits for them, and re-layouts: 2.53 us -> 3.95 us
  Pallas kernels: 26.1 us -> 27.5 us
  waiting for transfers between devices: 36.3 us -> 35.2 us
    pallas_call x0 -> x3, Pallas kernels: none -> 2.89 us  [the longest x1 1.41 us: ring_begins(): pl.pallas_call(kernel, out_shape=[jax.ShapeDtypeStruct((rows * RING, 128)...]
    pallas_call x1, Pallas kernels: 5.68 us -> 3.43 us  [attend_halo(): pl.pallas_call(kernel, out_shape=[jax.ShapeDtypeStruct((rows, part), jnp....]
    convert_element_type x2 -> x0, other arithmetic: 2.05 us -> none  [the longest x1 2.04 us: shards(): last = (conv_in[rows - TAPS:].astype(jnp.float32) * rms[rows - TAPS:, Non...]
    unnamed x24 -> x18, local copies, waits for them, and re-layouts: 1.97 us -> 3.95 us
    reduce_sum x1 -> x0, other arithmetic: 1.6 us -> none  [shards(): energy = lax.psum(jnp.sum(wide * wide, axis=1), 'ch')]
    ppermute x12, waiting for transfers between devices: 29 us -> 27.8 us  [ring_perm(): return lax.ppermute(value, 'seq', pairs)]
  transfers between devices with their start and end apart: 15 -> 15, of which waited for: 9 -> 9; matrix products, arithmetic and copies ran while one was open for 1% -> 0% of each run, Pallas kernels for 20% -> 22%
where the time goes in v3:
time: 98 us; the launch traced here: 96.4 us
  waiting for transfers between devices  35.2 us (36%)
  Pallas kernels  27.5 us (28%)
  starting transfers between devices  26.1 us (27%)
  local copies, waits for them, and re-layouts  3.95 us (4%)
  blocking collectives  2.6 us (3%)
  between operations  1.02 us (1%)
    ppermute x12, waiting for transfers between devices, ring_perm(): return lax.ppermute(value, 'seq', pairs)  27.8 us
    ppermute x12, starting transfers between devices, ring_perm(): return lax.ppermute(value, 'seq', pairs)  15.7 us
    ppermute x3, starting transfers between devices, ahead(): lax.ppermute(value, 'seq', [(i, i + step) for i in range(count - step)])  10.4 us
    ppermute x3, waiting for transfers between devices, ahead(): lax.ppermute(value, 'seq', [(i, i + step) for i in range(count - step)])  7.4 us
    pallas_call x1, Pallas kernels, convolve_own(): pl.pallas_call(kernel, out_shape=[jax.ShapeDtypeStruct((rows - TAPS, widt...  7.18 us
    pallas_call x1, Pallas kernels, attend_ring(): pl.pallas_call(kernel, out_shape=[jax.ShapeDtypeStruct((span, part), jnp....  6.25 us
    unnamed x18, local copies, waits for them, and re-layouts  3.95 us
    pallas_call x1, Pallas kernels, attend_halo(): pl.pallas_call(kernel, out_shape=[jax.ShapeDtypeStruct((rows, part), jnp....  3.43 us
  transfers between devices with their start and end apart: 15, of which 9 were waited for; matrix products, arithmetic and copies ran while one was open for 0% of the time, Pallas kernels for 22%

profile of v3, /device:TPU:128, one launch (start us, length us, event | category | flops | bytes accessed | tf_op | source)
XLA Modules:
  0.0 96.4 jit_solution(694063252360908975)
XLA Ops:
  0.6 0.0 copy-start.1
  0.6 0.0 copy-start.3
  0.6 1.3 %copy-done.3 = bf16[256,2048]{1,0:T(8,128)(2,1)S(1)} copy-done((bf16[256,2048]{1,0:T(8,128)(2,1)S(1)}, bf16[256,2048]{1,0:T(8,128)(2,1)}, u32[]{:S(2)}) %copy-start.3) | copy-done | bytes 1048600
  2.0 0.0 copy-start.7
  2.0 0.7 copy-done.7
  2.7 0.5 lead_in.1
  3.1 0.0 copy-start
  3.1 0.0 copy-start.6
  3.1 0.0 copy-start.8
  3.2 2.6 %psum.7.energy_ref = f32[2,128]{1,0:T(2,128)S(1)} all-reduce(f32[2,128]{1,0:T(2,128)S(1)} %get-tuple-element.46), channel_id=1, replica_groups=mesh['seq'=128,'ch'=2] {'ch'}, use_global_device_ids=true, to_apply=%region_0.0 | all-reduce | flops 256 | bytes 2048 | tf_op jit(solution)/shard_map/psum | solution.py:543
  5.8 1.0 %norm_last.1 = bf16[128,2048]{1,0:T(8,128)(2,1)} custom-call(bf16[256,2048]{1,0:T(8,128)(2,1)S(1)} %get-tuple-element.53.x_ref, f32[2,128]{1,0:T(2,128)S(1)} %psum.7.energy_ref, f32[1,2048]{1,0:T(1,128)S(1)} %get-tuple-element.54.gain_ref), custom_call_target="tpu_custom_call" | custom-call | tf_op jit(solution)/shard_map/norm_last/pallas_call | solution.py:183
  6.8 3.4 %collective-permute-start.3 = (bf16[128,2048]{1,0:T(8,128)(2,1)}, bf16[128,2048]{1,0:T(8,128)(2,1)}, u32[]{:S(2)}, u32[]{:S(2)}) collective-permute-start(bf16[128,2048]{1,0:T(8,128)(2,1)} %norm_last.1), channel_id=1, source_target_pairs={{0,2},{2,4},{4,6},{6,8},{8,10},{10,12},{12,14},{14,16},{16,18},{18... | collective-permute-start | bytes 1572872 | tf_op jit(solution)/shard_map/ppermute | solution.py:540
  10.2 0.0 copy-done.1
  10.2 0.0 copy-start.2
  10.2 1.2 %copy-done.2 = bf16[256,2048]{1,0:T(8,128)(2,1)S(1)} copy-done((bf16[256,2048]{1,0:T(8,128)(2,1)S(1)}, bf16[256,2048]{1,0:T(8,128)(2,1)}, u32[]{:S(2)}) %copy-start.2) | copy-done | bytes 1048600
  11.4 1.4 %quarters.1 = (bf16[256,512]{1,0:T(8,128)(2,1)S(1)}, bf16[256,512]{1,0:T(8,128)(2,1)}, bf16[256,512]{1,0:T(8,128)(2,1)}, bf16[256,512]{1,0:T(8,128)(2,1)}, bf16[...) custom-call(s32[1]{0:T(128)} %bitcast.place_ref, ...), custom_call_target="tpu_custom_call" | custom-call | tf_op jit(solution)/shard_map/quarters/pallas_call | solution.py:47
  12.8 0.0 copy-start.4
  12.9 0.7 copy-done.4
  13.6 1.5 %collective-permute-start = (bf16[256,512]{1,0:T(8,128)(2,1)}, bf16[256,512]{1,0:T(8,128)(2,1)S(1)}, u32[]{:S(2)}, u32[]{:S(2)}) collective-permute-start(bf16[256,512]{1,0:T(8,128)(2,1)} %get-tuple-element.50), channel_id=1, source_target_pairs={{0,2},{2,4},{4,6},{6,0},{8,10},{10,12},{12,14},{14,8},{16,18},{18,... | collective-permute-start | bytes 786440 | tf_op jit(solution)/shard_map/ppermute | solution.py:534
  15.0 2.7 %collective-permute-start.1 = (bf16[256,512]{1,0:T(8,128)(2,1)}, bf16[256,512]{1,0:T(8,128)(2,1)S(1)}, u32[]{:S(2)}, u32[]{:S(2)}) collective-permute-start(bf16[256,512]{1,0:T(8,128)(2,1)} %get-tuple-element.51), channel_id=1, source_target_pairs={{0,4},{2,6},{4,0},{6,2},{8,12},{10,14},{12,8},{14,10},{16,20},{18,... | collective-permute-start | bytes 786440 | tf_op jit(solution)/shard_map/ppermute | solution.py:534
  17.8 1.1 %collective-permute-start.2 = (bf16[256,512]{1,0:T(8,128)(2,1)}, bf16[256,512]{1,0:T(8,128)(2,1)S(1)}, u32[]{:S(2)}, u32[]{:S(2)}) collective-permute-start(bf16[256,512]{1,0:T(8,128)(2,1)} %get-tuple-element.52), channel_id=1, source_target_pairs={{0,6},{2,0},{4,2},{6,4},{8,14},{10,8},{12,10},{14,12},{16,22},{18,... | collective-permute-start | bytes 786440 | tf_op jit(solution)/shard_map/ppermute | solution.py:534
  18.9 0.0 copy-done
  18.9 0.0 copy-done.6
  18.9 0.0 copy-done.8
  18.9 7.2 %convolve_own.1 = (bf16[128,2048]{1,0:T(8,128)(2,1)S(1)}, f32[128,2048]{1,0:T(8,128)S(1)}, bf16[16,1024,128]{2,1,0:T(8,128)(2,1)S(1)}) custom-call(s32[1]{0:T(128)} %bitcast.2.base_ref, s32[48]{0:T(128)S(1)} %copy-done.8, bf16[256,2048]{1,0:T(8,128)(2,1)S(1)} %get-tuple-element.53.x_ref, f32[2,128]{1,0:T(2,128)S(1)} %psum.7.energy_ref, ...), custom_call_target="tpu_custom_call" | custom-call | tf_op jit(solution)/shard_map/convolve_own/pallas_call | solution.py:296
  26.1 2.4 %collective-permute-done.3.tail_ref = bf16[128,2048]{1,0:T(8,128)(2,1)} collective-permute-done((bf16[128,2048]{1,0:T(8,128)(2,1)}, bf16[128,2048]{1,0:T(8,128)(2,1)}, u32[]{:S(2)}, u32[]{:S(2)}) %collective-permute-start.3) | collective-permute-done | bytes 524320 | tf_op jit(solution)/shard_map/ppermute | solution.py:540
  28.5 3.4 %convolve_tail.1 = (bf16[256,2048]{1,0:T(8,128)(2,1)}, bf16[256,512]{1,0:T(8,128)(2,1)S(1)}, bf16[256,512]{1,0:T(8,128)(2,1)S(1)}, bf16[256,512]{1,0:T(8,128)(2,1)S(1)}, bf16[256,512]{1,0:T(8,128)(2,1)S(1)}) custom-call(s32[1]{0:T(128)} %bitcast.place_ref, bf16[128,2048]{1,0:T(8,128)(2,1)} %collective-permute-done.3.tail_ref, ...), custom_call_target="tpu_custom_call" | custom-call | tf_op jit(solution)/shard_map/convolve_tail/pallas_call | solution.py:346
  31.9 0.0 copy-start.5
  31.9 0.0 collective-permute-start.4
  31.9 0.0 collective-permute-start.5
  31.9 0.0 collective-permute-done.refs_5_.refs_1_
  31.9 3.2 %collective-permute-start.6 = (bf16[256,512]{1,0:T(8,128)(2,1)S(1)}, bf16[256,512]{1,0:T(8,128)(2,1)S(1)}, u32[]{:S(2)}, u32[]{:S(2)}) collective-permute-start(bf16[256,512]{1,0:T(8,128)(2,1)S(1)} %get-tuple-element.68), channel_id=1, source_target_pairs={{0,6},{2,0},{4,2},{6,4},{8,14},{10,8},{12,10},{14,12},{16,22},{18,... | collective-permute-start | bytes 786440 | tf_op jit(solution)/shard_map/ppermute | solution.py:534
  35.1 1.9 %collective-permute-done.1.refs_6_.refs_2_ = bf16[256,512]{1,0:T(8,128)(2,1)S(1)} collective-permute-done((bf16[256,512]{1,0:T(8,128)(2,1)}, bf16[256,512]{1,0:T(8,128)(2,1)S(1)}, u32[]{:S(2)}, u32[]{:S(2)}) %collective-permute-start.1) | collective-permute-done | bytes 262176 | tf_op jit(solution)/shard_map/ppermute | solution.py:534
  37.1 0.0 collective-permute-done.2.refs_7_.refs_3_
  37.1 1.0 %last_shards.3 = bf16[768,512]{1,0:T(8,128)(2,1)} custom-call(s32[1]{0:T(128)} %bitcast.place_ref, bf16[256,512]{1,0:T(8,128)(2,1)S(1)} %get-tuple-element.77.refs_4_.refs_0_, bf16[256,512]{1,0:T(8,128)(2,1)S(1)} %collective-permute-done.refs_5_.refs_1_, bf16[256,512]{1,0:T(8,128)(2,1)S(1)} %collective-permute-done.1.refs_6_.refs_2_, ...), custom_call_target="tpu_custom_call" | custom-call | tf_op jit(solution)/shard_map/last_shards/pallas_call | solution.py:116
  38.1 3.5 %collective-permute-start.10 = (bf16[768,512]{1,0:T(8,128)(2,1)}, bf16[768,512]{1,0:T(8,128)(2,1)S(1)}, u32[]{:S(2)}, u32[]{:S(2)}) collective-permute-start(bf16[768,512]{1,0:T(8,128)(2,1)} %last_shards.3), channel_id=1, source_target_pairs={{0,8},{2,10},{4,12},{6,14},{8,16},{10,18},{12,20},{14,22},{16,24},... | collective-permute-start | bytes 2359304 | tf_op jit(solution)/shard_map/ppermute | solution.py:540
  41.6 1.1 %collective-permute-done.4.refs_1_.refs_9_ = bf16[256,512]{1,0:T(8,128)(2,1)S(1)} collective-permute-done((bf16[256,512]{1,0:T(8,128)(2,1)S(1)}, bf16[256,512]{1,0:T(8,128)(2,1)S(1)}, u32[]{:S(2)}, u32[]{:S(2)}) %collective-permute-start.4) | collective-permute-done | bytes 262176 | tf_op jit(solution)/shard_map/ppermute | solution.py:534
  42.7 4.8 %collective-permute-done.5.refs_2_.refs_10_ = bf16[256,512]{1,0:T(8,128)(2,1)S(1)} collective-permute-done((bf16[256,512]{1,0:T(8,128)(2,1)S(1)}, bf16[256,512]{1,0:T(8,128)(2,1)S(1)}, u32[]{:S(2)}, u32[]{:S(2)}) %collective-permute-start.5) | collective-permute-done | bytes 262176 | tf_op jit(solution)/shard_map/ppermute | solution.py:534
  47.6 0.0 collective-permute-done.6.refs_3_.refs_11_
  47.6 1.0 %last_shards.2 = bf16[768,512]{1,0:T(8,128)(2,1)} custom-call(s32[1]{0:T(128)} %bitcast.place_ref, bf16[256,512]{1,0:T(8,128)(2,1)S(1)} %get-tuple-element.65.refs_0_.refs_8_, bf16[256,512]{1,0:T(8,128)(2,1)S(1)} %collective-permute-done.4.refs_1_.refs_9_, bf16[256,512]{1,0:T(8,128)(2,1)S(1)} %collective-permute-done.5.refs_2_.refs_10_, ...), custom_call_target="tpu_custom_call" | custom-call | tf_op jit(solution)/shard_map/last_shards/pallas_call | solution.py:116
  48.6 3.5 %collective-permute-start.11 = (bf16[768,512]{1,0:T(8,128)(2,1)}, bf16[768,512]{1,0:T(8,128)(2,1)}, u32[]{:S(2)}, u32[]{:S(2)}) collective-permute-start(bf16[768,512]{1,0:T(8,128)(2,1)} %last_shards.2), channel_id=1, source_target_pairs={{0,8},{2,10},{4,12},{6,14},{8,16},{10,18},{12,20},{14,22},{16,24},... | collective-permute-start | bytes 2359304 | tf_op jit(solution)/shard_map/ppermute | solution.py:540
  52.1 0.1 collective-permute-start.7
  52.2 1.5 %collective-permute-start.8 = (bf16[256,512]{1,0:T(8,128)(2,1)}, bf16[256,512]{1,0:T(8,128)(2,1)}, u32[]{:S(2)}, u32[]{:S(2)}) collective-permute-start(bf16[256,512]{1,0:T(8,128)(2,1)} %get-tuple-element.75), channel_id=1, source_target_pairs={{0,4},{2,6},{4,0},{6,2},{8,12},{10,14},{12,8},{14,10},{16,20},{18,... | collective-permute-start | bytes 786440 | tf_op jit(solution)/shard_map/ppermute | solution.py:534
  53.7 1.9 %collective-permute-start.9 = (bf16[256,512]{1,0:T(8,128)(2,1)}, bf16[256,512]{1,0:T(8,128)(2,1)}, u32[]{:S(2)}, u32[]{:S(2)}) collective-permute-start(bf16[256,512]{1,0:T(8,128)(2,1)} %get-tuple-element.76), channel_id=1, source_target_pairs={{0,6},{2,0},{4,2},{6,4},{8,14},{10,8},{12,10},{14,12},{16,22},{18,... | collective-permute-start | bytes 786440 | tf_op jit(solution)/shard_map/ppermute | solution.py:534
  55.6 1.4 %ring_begins.1 = (s32[1024,128]{1,0:T(8,128)S(1)}, s32[4]{0:T(128)S(1)}) custom-call(s32[48]{0:T(128)S(1)} %copy-done.8, s32[1]{0:T(128)} %bitcast.3.base_ref), custom_call_target="tpu_custom_call" | custom-call | tf_op jit(solution)/shard_map/ring_begins/pallas_call | solution.py:220
  57.0 9.4 %collective-permute-done.7.refs_1_ = bf16[256,512]{1,0:T(8,128)(2,1)S(1)} collective-permute-done((bf16[256,512]{1,0:T(8,128)(2,1)}, bf16[256,512]{1,0:T(8,128)(2,1)S(1)}, u32[]{:S(2)}, u32[]{:S(2)}) %collective-permute-start.7) | collective-permute-done | bytes 262176 | tf_op jit(solution)/shard_map/ppermute | solution.py:534
  66.5 0.0 collective-permute-done.8.refs_2_
  66.5 0.7 collective-permute-done.9.refs_3_
  67.2 0.0 copy-done.5
  67.2 6.3 %attend_ring.1 = (f32[1024,512]{1,0:T(8,128)S(1)}, f32[1024,512]{1,0:T(8,128)S(1)}, f32[1024,512]{1,0:T(8,128)S(1)}, bf16[1024,512]{1,0:T(8,128)(2,1)S(1)}) custom-call(s32[1]{0:T(128)} %bitcast.place_ref, s32[1024,128]{1,0:T(8,128)S(1)} %get-tuple-element.64.begin_ref, bf16[256,512]{1,0:T(8,128)(2,1)S(1)} %copy-done.5, ...), custom_call_target="tpu_custom_call" | custom-call | tf_op jit(solution)/shard_map/attend_ring/pallas_call | solution.py:417
  73.5 0.0 collective-permute-done.10.k_ref
  73.5 5.0 %collective-permute-done.11.v_ref = bf16[768,512]{1,0:T(8,128)(2,1)} collective-permute-done((bf16[768,512]{1,0:T(8,128)(2,1)}, bf16[768,512]{1,0:T(8,128)(2,1)}, u32[]{:S(2)}, u32[]{:S(2)}) %collective-permute-start.11) | collective-permute-done | bytes 786464 | tf_op jit(solution)/shard_map/ppermute | solution.py:540
  78.5 3.4 %attend_halo.1 = (bf16[256,512]{1,0:T(8,128)(2,1)S(1)}, bf16[256,512]{1,0:T(8,128)(2,1)S(1)}, bf16[256,512]{1,0:T(8,128)(2,1)S(1)}, bf16[256,512]{1,0:T(8,128)(2,1)S(1)}) custom-call(s32[1]{0:T(128)} %bitcast.place_ref, s32[4]{0:T(128)S(1)} %get-tuple-element.63.edge_ref, s32[1024,128]{1,0:T(8,128)S(1)} %get-tuple-element.64.begin_ref, ...), custom_call_target="tpu_custom_call" | custom-call | tf_op jit(solution)/shard_map/attend_halo/pallas_call | solution.py:507
  81.9 0.1 collective-permute-start.12
  82.0 1.0 %collective-permute-start.13 = (bf16[256,512]{1,0:T(8,128)(2,1)S(1)}, bf16[256,512]{1,0:T(8,128)(2,1)S(1)}, u32[]{:S(2)}, u32[]{:S(2)}) collective-permute-start(bf16[256,512]{1,0:T(8,128)(2,1)S(1)} %get-tuple-element.88), channel_id=1, source_target_pairs={{0,4},{2,6},{4,0},{6,2},{8,12},{10,14},{12,8},{14,10},{16,20},{18,... | collective-permute-start | bytes 786440 | tf_op jit(solution)/shard_map/ppermute | solution.py:534
  83.0 2.5 %collective-permute-start.14 = (bf16[256,512]{1,0:T(8,128)(2,1)S(1)}, bf16[256,512]{1,0:T(8,128)(2,1)S(1)}, u32[]{:S(2)}, u32[]{:S(2)}) collective-permute-start(bf16[256,512]{1,0:T(8,128)(2,1)S(1)} %get-tuple-element.89), channel_id=1, source_target_pairs={{0,6},{2,0},{4,2},{6,4},{8,14},{10,8},{12,10},{14,12},{16,22},{18,... | collective-permute-start | bytes 786440 | tf_op jit(solution)/shard_map/ppermute | solution.py:534
  85.5 9.2 %collective-permute-done.12.refs_1_ = bf16[256,512]{1,0:T(8,128)(2,1)S(1)} collective-permute-done((bf16[256,512]{1,0:T(8,128)(2,1)S(1)}, bf16[256,512]{1,0:T(8,128)(2,1)S(1)}, u32[]{:S(2)}, u32[]{:S(2)}) %collective-permute-start.12) | collective-permute-done | bytes 262176 | tf_op jit(solution)/shard_map/ppermute | solution.py:534
  94.6 0.0 collective-permute-done.13.refs_2_
  94.7 0.6 collective-permute-done.14.refs_3_
  95.3 1.0 %whole_width.1 = bf16[256,2048]{1,0:T(8,128)(2,1)} custom-call(s32[1]{0:T(128)} %bitcast.place_ref, bf16[256,512]{1,0:T(8,128)(2,1)S(1)} %get-tuple-element.86.refs_0_, bf16[256,512]{1,0:T(8,128)(2,1)S(1)} %collective-permute-done.12.refs_1_, bf16[256,512]{1,0:T(8,128)(2,1)S(1)} %collective-permute-done.13.refs_2_, ...), custom_call_target="tpu_custom_call" | custom-call | tf_op jit(solution)/shard_map/whole_width/pallas_call | solution.py:80
Async XLA Ops:
  0.6 9.6 %copy-start.1 = (bf16[256,2048]{1,0:T(8,128)(2,1)S(1)}, bf16[256,2048]{1,0:T(8,128)(2,1)}, u32[]{:S(2)}) copy-start(bf16[256,2048]{1,0:T(8,128)(2,1)} %refs_0_) | copy-start | bytes 3145732
  0.6 1.3 %copy-start.3 = (bf16[256,2048]{1,0:T(8,128)(2,1)S(1)}, bf16[256,2048]{1,0:T(8,128)(2,1)}, u32[]{:S(2)}) copy-start(bf16[256,2048]{1,0:T(8,128)(2,1)} %x_hbm.1) | copy-start | bytes 3145732
  2.0 0.7 copy-start.7
  3.1 15.8 %copy-start = (bf16[256,2048]{1,0:T(8,128)(2,1)S(1)}, bf16[256,2048]{1,0:T(8,128)(2,1)}, u32[]{:S(2)}) copy-start(bf16[256,2048]{1,0:T(8,128)(2,1)} %gate_ref.3) | copy-start | bytes 3145732
  3.1 15.8 %copy-start.6 = (bf16[128,128]{1,0:T(8,128)(2,1)S(1)}, bf16[128,128]{1,0:T(8,128)(2,1)}, u32[]{:S(2)}) copy-start(bf16[128,128]{1,0:T(8,128)(2,1)} %filter_ref.1) | copy-start | bytes 98308
  3.1 15.8 %copy-start.8 = (s32[48]{0:T(128)S(1)}, s32[48]{0:T(128)}, u32[]{:S(2)}) copy-start(s32[48]{0:T(128)} %lengths_ref.2) | copy-start | bytes 580
  6.8 21.7 %collective-permute-start.3 = (bf16[128,2048]{1,0:T(8,128)(2,1)}, bf16[128,2048]{1,0:T(8,128)(2,1)}, u32[]{:S(2)}, u32[]{:S(2)}) collective-permute-start(bf16[128,2048]{1,0:T(8,128)(2,1)} %norm_last.1), channel_id=1, source_target_pairs={{0,2},{2,4},{4,6},{6,8},{8,10},{10,12},{12,14},{14,16},{16,18},{18... | collective-permute-start | bytes 1572872 | tf_op jit(solution)/shard_map/ppermute | solution.py:540
  10.2 1.2 %copy-start.2 = (bf16[256,2048]{1,0:T(8,128)(2,1)S(1)}, bf16[256,2048]{1,0:T(8,128)(2,1)}, u32[]{:S(2)}) copy-start(bf16[256,2048]{1,0:T(8,128)(2,1)} %refs_1_) | copy-start | bytes 3145732
  12.8 0.7 copy-start.4
  13.6 18.4 %collective-permute-start = (bf16[256,512]{1,0:T(8,128)(2,1)}, bf16[256,512]{1,0:T(8,128)(2,1)S(1)}, u32[]{:S(2)}, u32[]{:S(2)}) collective-permute-start(bf16[256,512]{1,0:T(8,128)(2,1)} %get-tuple-element.50), channel_id=1, source_target_pairs={{0,2},{2,4},{4,6},{6,0},{8,10},{10,12},{12,14},{14,8},{16,18},{18,... | collective-permute-start | bytes 786440 | tf_op jit(solution)/shard_map/ppermute | solution.py:534
  15.0 22.0 %collective-permute-start.1 = (bf16[256,512]{1,0:T(8,128)(2,1)}, bf16[256,512]{1,0:T(8,128)(2,1)S(1)}, u32[]{:S(2)}, u32[]{:S(2)}) collective-permute-start(bf16[256,512]{1,0:T(8,128)(2,1)} %get-tuple-element.51), channel_id=1, source_target_pairs={{0,4},{2,6},{4,0},{6,2},{8,12},{10,14},{12,8},{14,10},{16,20},{18,... | collective-permute-start | bytes 786440 | tf_op jit(solution)/shard_map/ppermute | solution.py:534
  17.8 19.3 %collective-permute-start.2 = (bf16[256,512]{1,0:T(8,128)(2,1)}, bf16[256,512]{1,0:T(8,128)(2,1)S(1)}, u32[]{:S(2)}, u32[]{:S(2)}) collective-permute-start(bf16[256,512]{1,0:T(8,128)(2,1)} %get-tuple-element.52), channel_id=1, source_target_pairs={{0,6},{2,0},{4,2},{6,4},{8,14},{10,8},{12,10},{14,12},{16,22},{18,... | collective-permute-start | bytes 786440 | tf_op jit(solution)/shard_map/ppermute | solution.py:534
  31.9 35.3 %copy-start.5 = (bf16[256,512]{1,0:T(8,128)(2,1)S(1)}, bf16[256,512]{1,0:T(8,128)(2,1)}, u32[]{:S(2)}) copy-start(bf16[256,512]{1,0:T(8,128)(2,1)} %copy-done.4) | copy-start | bytes 786436
  31.9 10.8 %collective-permute-start.4 = (bf16[256,512]{1,0:T(8,128)(2,1)S(1)}, bf16[256,512]{1,0:T(8,128)(2,1)S(1)}, u32[]{:S(2)}, u32[]{:S(2)}) collective-permute-start(bf16[256,512]{1,0:T(8,128)(2,1)S(1)} %get-tuple-element.66), channel_id=1, source_target_pairs={{0,2},{2,4},{4,6},{6,0},{8,10},{10,12},{12,14},{14,8},{16,18},{18,... | collective-permute-start | bytes 786440 | tf_op jit(solution)/shard_map/ppermute | solution.py:534
  31.9 15.7 %collective-permute-start.5 = (bf16[256,512]{1,0:T(8,128)(2,1)S(1)}, bf16[256,512]{1,0:T(8,128)(2,1)S(1)}, u32[]{:S(2)}, u32[]{:S(2)}) collective-permute-start(bf16[256,512]{1,0:T(8,128)(2,1)S(1)} %get-tuple-element.67), channel_id=1, source_target_pairs={{0,4},{2,6},{4,0},{6,2},{8,12},{10,14},{12,8},{14,10},{16,20},{18,... | collective-permute-start | bytes 786440 | tf_op jit(solution)/shard_map/ppermute | solution.py:534
  31.9 15.6 %collective-permute-start.6 = (bf16[256,512]{1,0:T(8,128)(2,1)S(1)}, bf16[256,512]{1,0:T(8,128)(2,1)S(1)}, u32[]{:S(2)}, u32[]{:S(2)}) collective-permute-start(bf16[256,512]{1,0:T(8,128)(2,1)S(1)} %get-tuple-element.68), channel_id=1, source_target_pairs={{0,6},{2,0},{4,2},{6,4},{8,14},{10,8},{12,10},{14,12},{16,22},{18,... | collective-permute-start | bytes 786440 | tf_op jit(solution)/shard_map/ppermute | solution.py:534
  38.1 35.4 %collective-permute-start.10 = (bf16[768,512]{1,0:T(8,128)(2,1)}, bf16[768,512]{1,0:T(8,128)(2,1)S(1)}, u32[]{:S(2)}, u32[]{:S(2)}) collective-permute-start(bf16[768,512]{1,0:T(8,128)(2,1)} %last_shards.3), channel_id=1, source_target_pairs={{0,8},{2,10},{4,12},{6,14},{8,16},{10,18},{12,20},{14,22},{16,24},... | collective-permute-start | bytes 2359304 | tf_op jit(solution)/shard_map/ppermute | solution.py:540
  48.6 29.9 %collective-permute-start.11 = (bf16[768,512]{1,0:T(8,128)(2,1)}, bf16[768,512]{1,0:T(8,128)(2,1)}, u32[]{:S(2)}, u32[]{:S(2)}) collective-permute-start(bf16[768,512]{1,0:T(8,128)(2,1)} %last_shards.2), channel_id=1, source_target_pairs={{0,8},{2,10},{4,12},{6,14},{8,16},{10,18},{12,20},{14,22},{16,24},... | collective-permute-start | bytes 2359304 | tf_op jit(solution)/shard_map/ppermute | solution.py:540
  52.1 14.4 %collective-permute-start.7 = (bf16[256,512]{1,0:T(8,128)(2,1)}, bf16[256,512]{1,0:T(8,128)(2,1)S(1)}, u32[]{:S(2)}, u32[]{:S(2)}) collective-permute-start(bf16[256,512]{1,0:T(8,128)(2,1)} %get-tuple-element.74), channel_id=1, source_target_pairs={{0,2},{2,4},{4,6},{6,0},{8,10},{10,12},{12,14},{14,8},{16,18},{18,... | collective-permute-start | bytes 786440 | tf_op jit(solution)/shard_map/ppermute | solution.py:534
  52.2 14.3 %collective-permute-start.8 = (bf16[256,512]{1,0:T(8,128)(2,1)}, bf16[256,512]{1,0:T(8,128)(2,1)}, u32[]{:S(2)}, u32[]{:S(2)}) collective-permute-start(bf16[256,512]{1,0:T(8,128)(2,1)} %get-tuple-element.75), channel_id=1, source_target_pairs={{0,4},{2,6},{4,0},{6,2},{8,12},{10,14},{12,8},{14,10},{16,20},{18,... | collective-permute-start | bytes 786440 | tf_op jit(solution)/shard_map/ppermute | solution.py:534
  53.7 13.5 %collective-permute-start.9 = (bf16[256,512]{1,0:T(8,128)(2,1)}, bf16[256,512]{1,0:T(8,128)(2,1)}, u32[]{:S(2)}, u32[]{:S(2)}) collective-permute-start(bf16[256,512]{1,0:T(8,128)(2,1)} %get-tuple-element.76), channel_id=1, source_target_pairs={{0,6},{2,0},{4,2},{6,4},{8,14},{10,8},{12,10},{14,12},{16,22},{18,... | collective-permute-start | bytes 786440 | tf_op jit(solution)/shard_map/ppermute | solution.py:534
  81.9 12.8 %collective-permute-start.12 = (bf16[256,512]{1,0:T(8,128)(2,1)S(1)}, bf16[256,512]{1,0:T(8,128)(2,1)S(1)}, u32[]{:S(2)}, u32[]{:S(2)}) collective-permute-start(bf16[256,512]{1,0:T(8,128)(2,1)S(1)} %get-tuple-element.87), channel_id=1, source_target_pairs={{0,2},{2,4},{4,6},{6,0},{8,10},{10,12},{12,14},{14,8},{16,18},{18,... | collective-permute-start | bytes 786440 | tf_op jit(solution)/shard_map/ppermute | solution.py:534
  82.0 12.7 %collective-permute-start.13 = (bf16[256,512]{1,0:T(8,128)(2,1)S(1)}, bf16[256,512]{1,0:T(8,128)(2,1)S(1)}, u32[]{:S(2)}, u32[]{:S(2)}) collective-permute-start(bf16[256,512]{1,0:T(8,128)(2,1)S(1)} %get-tuple-element.88), channel_id=1, source_target_pairs={{0,4},{2,6},{4,0},{6,2},{8,12},{10,14},{12,8},{14,10},{16,20},{18,... | collective-permute-start | bytes 786440 | tf_op jit(solution)/shard_map/ppermute | solution.py:534
  83.0 12.3 %collective-permute-start.14 = (bf16[256,512]{1,0:T(8,128)(2,1)S(1)}, bf16[256,512]{1,0:T(8,128)(2,1)S(1)}, u32[]{:S(2)}, u32[]{:S(2)}) collective-permute-start(bf16[256,512]{1,0:T(8,128)(2,1)S(1)} %get-tuple-element.89), channel_id=1, source_target_pairs={{0,6},{2,0},{4,2},{6,4},{8,14},{10,8},{12,10},{14,12},{16,22},{18,... | collective-permute-start | bytes 786440 | tf_op jit(solution)/shard_map/ppermute | solution.py:534
